TPU v7x, 512 devices: a whole 4x4x16 slice. The times are simulated.
512 devices in a mesh: expert: 128 (over y, z, core), half: 4 (over x).
Axes of the slice: x: 4, y: 4, z: 16, core: 2. Of those that a mesh axis runs over, the one named last changes fastest.
Arguments:
- tokens: bfloat16 [2048, 2048], P('expert', 'half'), may hold values from -6 to 6
- upstream: bfloat16 [2048, 2048], P('expert', 'half'), may hold values from -6 to 6
- expert_ids: int32 [2048, 8], P('expert'), may hold values from 0 to 127, all different within a row; in each aligned block of 16 rows (0 to 15, 16 to 31, ...) at most 2 rows name the same one
- gate_probs: float32 [2048, 8], P('expert'), may hold values from 0.01 to 1
- pad_mask: int32 [2048], P('expert'), may hold values 0 or 1
- gate_weight: bfloat16 [128, 2048, 1536], P('expert', None, 'half'), may hold values from -0.125 to 0.125
- up_weight: bfloat16 [128, 2048, 1536], P('expert', None, 'half'), may hold values from -0.125 to 0.125
- down_weight: bfloat16 [128, 1536, 2048], P('expert', 'half'), may hold values from -0.15625 to 0.15625
Outputs:
- layer_out: bfloat16 [2048, 2048], P('expert', 'half')
- grad_tokens: bfloat16 [2048, 2048], P('expert', 'half')
Inputs may be any that keep to these rules, and one draw needn't show every extreme that they name: `expert_ids`: each row names 8 different experts. In the rows of one device (aligned blocks of 16 rows) no expert is named more than 2 times, a bound that some block reaches.
All inputs are finite; a program needn't handle non-finite values. No bound on the sum of `pad_mask` on one device may be relied on, other than what follows from the above.
Results may differ from a plain program's by a relative error of at most 0.025.
Values may be sent and summed in bfloat16 or wider, within the bound.
No kernel may reach another device: no remote copies, remote signals or barrier semaphores. Data moves between devices by JAX's collectives and lax.ppermute only.
A program may use at most 64 MiB of HBM per device.

v0:
```python
import math

import jax
import jax.numpy as jnp
from jax import lax
from jax.sharding import PartitionSpec as P

orth_weight = 0.25


def assign_slots(expert_ids, experts, capacity):
    tok_count, top_count = expert_ids.shape
    flat_ids = expert_ids.reshape(tok_count * top_count)
    onehot = (flat_ids[:, None] == jnp.arange(experts, dtype=jnp.int32)[None, :]).astype(jnp.int32)
    before = jnp.cumsum(onehot, axis=0) - onehot
    slot_index = jnp.sum(before * onehot, axis=1)
    return flat_ids * capacity + slot_index


def placement_matrix(slot_dest, slots_total):
    row_index = jnp.arange(slots_total, dtype=jnp.int32)
    return (row_index[:, None] == slot_dest[None, :]).astype(jnp.bfloat16)


def to_experts(place, items):
    whole = lax.all_gather(items, "half", axis=1, tiled=True)
    buckets = jnp.dot(place, whole, preferred_element_type=jnp.float32).astype(jnp.bfloat16)
    return lax.all_to_all(buckets, "expert", split_axis=0, concat_axis=0, tiled=True)


def to_homes(partial_value):
    summed = lax.psum_scatter(
        partial_value.astype(jnp.bfloat16), "half", scatter_dimension=1, tiled=True
    )
    return lax.all_to_all(summed, "expert", split_axis=0, concat_axis=0, tiled=True)


def shards(tokens, upstream, expert_ids, gate_probs, pad_mask, gate_weight, up_weight, down_weight):
    tok_count, top_count = expert_ids.shape
    experts = lax.axis_size("expert")
    capacity = min(tok_count, 2 * tok_count * top_count // experts)
    slots_total = experts * capacity
    full_width = tokens.shape[1] * lax.axis_size("half")
    slot_dest = assign_slots(expert_ids, experts, capacity)
    place_items = placement_matrix(slot_dest, slots_total)
    place_tokens = jnp.sum(place_items.reshape(slots_total, tok_count, top_count), axis=2)
    weight_gate = gate_weight[0]
    weight_up = up_weight[0]
    weight_down = down_weight[0]
    rows_in = to_experts(place_tokens, tokens)
    gate_val = jnp.dot(rows_in, weight_gate, preferred_element_type=jnp.float32)
    up_val = jnp.dot(rows_in, weight_up, preferred_element_type=jnp.float32)
    hidden_act = (jax.nn.silu(gate_val) * up_val).astype(jnp.bfloat16)
    partial_value = jnp.dot(hidden_act, weight_down, preferred_element_type=jnp.float32)
    out_home = to_homes(partial_value)
    outputs = jnp.take(out_home, slot_dest, axis=0).reshape(tok_count, top_count, -1)
    out_float = outputs.astype(jnp.float32)
    shares = gate_probs / jnp.sum(gate_probs, axis=1, keepdims=True)
    layer_out = jnp.sum(shares[:, :, None] * out_float, axis=1).astype(jnp.bfloat16)
    gram_part = jnp.einsum("tjd,tkd->tjk", out_float, out_float) / math.sqrt(full_width)
    gram = lax.psum(gram_part, "half")
    off_diag = 1.0 - jnp.eye(top_count, dtype=jnp.float32)
    coeffs = orth_weight * gram * off_diag
    grad_out = pad_mask.astype(jnp.float32)[:, None, None] * (
        shares[:, :, None] * upstream.astype(jnp.float32)[:, None, :]
        + jnp.einsum("tjk,tkd->tjd", coeffs, out_float)
    )
    grad_items = grad_out.astype(jnp.bfloat16).reshape(tok_count * top_count, -1)
    grad_rows = to_experts(place_items, grad_items)
    grad_act = jnp.einsum("rd,hd->rh", grad_rows, weight_down, preferred_element_type=jnp.float32)
    sigma = jax.nn.sigmoid(gate_val)
    grad_gate = (grad_act * up_val * sigma * (1.0 + gate_val * (1.0 - sigma))).astype(jnp.bfloat16)
    grad_up = (grad_act * gate_val * sigma).astype(jnp.bfloat16)
    grad_partial = jnp.einsum(
        "rh,dh->rd", grad_gate, weight_gate, preferred_element_type=jnp.float32
    )
    grad_partial = grad_partial + jnp.einsum(
        "rh,dh->rd", grad_up, weight_up, preferred_element_type=jnp.float32
    )
    grad_home = to_homes(grad_partial)
    grad_pairs = jnp.take(grad_home, slot_dest, axis=0).reshape(tok_count, top_count, -1)
    grad_tokens = jnp.sum(grad_pairs.astype(jnp.float32), axis=1).astype(jnp.bfloat16)
    return (layer_out, grad_tokens)


def solution(mesh):
    in_specs = (
        P("expert", "half"),
        P("expert", "half"),
        P("expert", None),
        P("expert", None),
        P("expert"),
        P("expert", None, "half"),
        P("expert", None, "half"),
        P("expert", "half", None),
    )
    out_specs = (P("expert", "half"), P("expert", "half"))
    return jax.shard_map(shards, mesh=mesh, in_specs=in_specs, out_specs=out_specs, check_vma=False)
```

profile of v0, /device:TPU:1, one launch (start us, length us, event | category | flops | bytes accessed | tf_op | source)
XLA Modules:
  0.0 342.9 jit_solution(6629864669466501402)
XLA Ops:
  7.2 0.9 copy.17
  8.9 10.4 %all_gather.6 = bf16[16,2048]{1,0:T(8,128)(2,1)S(1)} all-gather(bf16[16,512]{1,0:T(8,128)(2,1)} %param.10), channel_id=1, replica_groups=mesh['expert'=128,'half'=4] {'half'}, dimensions={1}, use_global_device_ids=true | all-gather | bytes 81920 | tf_op jit(solution)/shard_map/all_gather | solution.py:26
  19.2 0.5 convolution_convert_fusion.2
  19.7 1.5 all_to_all.32
  21.2 77.1 %all_to_all.48 = bf16[128,2,2048]{2,1,0:T(2,128)(2,1)} all-to-all(bf16[128,2,2048]{2,1,0:T(2,128)(2,1)} %all_to_all.32), channel_id=1, replica_groups=mesh['expert'=128,'half'=4] {'expert'}, dimensions={0} | all-to-all | bytes 2097152 | tf_op jit(solution)/shard_map/all_to_all | solution.py:28
  98.3 1.5 all_to_all.34
  99.8 2.2 fusion.9
  102.0 0.7 fusion.5
  102.7 1.7 convolution_convert_fusion.1
  104.5 22.2 %reduce-scatter.3.cloned.1.call-done = bf16[256,512]{1,0:T(8,128)(2,1)} async-done(((bf16[256,2048]{1,0:T(8,128)(2,1)}), bf16[256,512]{1,0:T(8,128)(2,1)}) %reduce-scatter.3.cloned.1.call-update) | async-done | bytes 262160 | tf_op jit(solution)/shard_map/reduce_scatter | solution.py:32
  126.7 1.7 all_to_all.35
  128.4 18.4 %all-to-all-start.1 = ((bf16[128,2,512]{2,1,0:T(2,128)(2,1)}), bf16[128,2,512]{2,1,0:T(2,128)(2,1)S(1)}, u32[]{:S(2)}, u32[]{:S(2)}) async-start(bf16[128,2,512]{2,1,0:T(2,128)(2,1)} %all_to_all.35), calls=%async_computation.2 | async-start | bytes 524288 | tf_op jit(solution)/shard_map/all_to_all | solution.py:35
  147.1 22.2 %all-to-all-done.1 = bf16[128,2,512]{2,1,0:T(2,128)(2,1)S(1)} async-done(((bf16[128,2,512]{2,1,0:T(2,128)(2,1)}), bf16[128,2,512]{2,1,0:T(2,128)(2,1)S(1)}, u32[]{:S(2)}, u32[]{:S(2)}) %all-to-all-start.1) | async-done | bytes 262176 | tf_op jit(solution)/shard_map/all_to_all | solution.py:35
  169.4 0.8 gather_fusion
  170.5 11.8 %psum.7 = f32[16,8,8]{2,1,0:T(8,128)S(1)} all-reduce(f32[16,8,8]{2,1,0:T(8,128)S(1)} %convolution_multiply_fusion), channel_id=1, replica_groups=mesh['expert'=128,'half'=4] {'half'}, use_global_device_ids=true, to_apply=%region_6.8 | all-reduce | flops 1024 | bytes 8192 | tf_op jit(solution)/shard_map/psum | solution.py:61
  182.6 10.1 %all_gather.7 = bf16[128,2048]{1,0:T(8,128)(2,1)S(1)} all-gather(bf16[128,512]{1,0:T(8,128)(2,1)S(1)} %fusion.13), channel_id=1, replica_groups=mesh['expert'=128,'half'=4] {'half'}, dimensions={1}, use_global_device_ids=true | all-gather | bytes 655360 | tf_op jit(solution)/shard_map/all_gather | solution.py:26
  192.7 1.1 convolution_convert_fusion
  193.8 1.5 all_to_all.38
  195.3 69.1 %all_to_all.49 = bf16[128,2,2048]{2,1,0:T(2,128)(2,1)} all-to-all(bf16[128,2,2048]{2,1,0:T(2,128)(2,1)} %all_to_all.38), channel_id=1, replica_groups=mesh['expert'=128,'half'=4] {'expert'}, dimensions={0} | all-to-all | bytes 2097152 | tf_op jit(solution)/shard_map/all_to_all | solution.py:28
  264.4 1.5 all_to_all.40
  265.9 0.7 fusion.1
  266.6 0.7 copy-done.1
  267.3 0.8 fusion.7
  268.1 0.6 copy-done.3
  268.7 1.8 fusion
  270.5 20.9 %reduce-scatter.5.cloned.1.call-done = bf16[256,512]{1,0:T(8,128)(2,1)} async-done(((bf16[256,2048]{1,0:T(8,128)(2,1)}), bf16[256,512]{1,0:T(8,128)(2,1)}) %reduce-scatter.5.cloned.1.call-update) | async-done | bytes 262160 | tf_op jit(solution)/shard_map/reduce_scatter | solution.py:32
  291.4 1.7 all_to_all.41
  293.2 18.7 %all-to-all-start.3 = ((bf16[128,2,512]{2,1,0:T(2,128)(2,1)}), bf16[128,2,512]{2,1,0:T(2,128)(2,1)S(1)}, u32[]{:S(2)}, u32[]{:S(2)}) async-start(bf16[128,2,512]{2,1,0:T(2,128)(2,1)} %all_to_all.41), calls=%async_computation.5 | async-start | bytes 524288 | tf_op jit(solution)/shard_map/all_to_all | solution.py:35
  311.9 0.8 multiply_reduce_fusion
  312.6 21.7 %all-to-all-done.3 = bf16[128,2,512]{2,1,0:T(2,128)(2,1)S(1)} async-done(((bf16[128,2,512]{2,1,0:T(2,128)(2,1)}), bf16[128,2,512]{2,1,0:T(2,128)(2,1)S(1)}, u32[]{:S(2)}, u32[]{:S(2)}) %all-to-all-start.3) | async-done | bytes 262176 | tf_op jit(solution)/shard_map/all_to_all | solution.py:35
  334.5 0.8 gather_fusion.1
  335.3 0.7 bitcast_reduce_fusion
  (38 shorter events, 1.7 us)
Async XLA Ops:
  7.2 95.6 %copy-start = (bf16[1,384,2048]{2,1,0:T(8,128)(2,1)S(1)}, bf16[1,384,2048]{2,1,0:T(8,128)(2,1)}, u32[]{:S(2)}) copy-start(bf16[1,384,2048]{2,1,0:T(8,128)(2,1)} %param.17) | copy-start | bytes 4718596
  7.2 119.5 %reduce-scatter.3.cloned.1.call-start = ((), (), s32[]{:S(2)}) async-start(), calls=%async_computation.6 | async-start | bytes 1310720 | tf_op jit(solution)/shard_map/reduce_scatter | solution.py:32
  99.8 2.2 copy-start.2
  104.5 42.4 %copy-start.7 = (s32[16]{0:T(128)S(1)}, s32[16]{0:T(128)}, u32[]{:S(2)}) copy-start(s32[16]{0:T(128)} %param.14) | copy-start | bytes 196
  104.5 42.4 %copy-start.5 = (f32[16,8]{0,1:T(8,128)S(1)}, f32[16,8]{0,1:T(8,128)}, u32[]{:S(2)}) copy-start(f32[16,8]{0,1:T(8,128)} %param.13) | copy-start | bytes 1540
  104.5 42.5 %copy-start.4 = (bf16[16,512]{1,0:T(8,128)(2,1)S(1)}, bf16[16,512]{1,0:T(8,128)(2,1)}, u32[]{:S(2)}) copy-start(bf16[16,512]{1,0:T(8,128)(2,1)} %param.11) | copy-start | bytes 49156
  128.4 40.9 %all-to-all-start.1 = ((bf16[128,2,512]{2,1,0:T(2,128)(2,1)}), bf16[128,2,512]{2,1,0:T(2,128)(2,1)S(1)}, u32[]{:S(2)}, u32[]{:S(2)}) async-start(bf16[128,2,512]{2,1,0:T(2,128)(2,1)} %all_to_all.35), calls=%async_computation.2 | async-start | bytes 524288 | tf_op jit(solution)/shard_map/all_to_all | solution.py:35
  146.8 144.6 %reduce-scatter.5.cloned.1.call-start = ((), (), s32[]{:S(2)}) async-start(), calls=%async_computation.7 | async-start | bytes 1310720 | tf_op jit(solution)/shard_map/reduce_scatter | solution.py:32
  147.0 22.3 %copy-start.6 = (s32[128]{0:T(128)}, s32[128]{0:T(128)S(1)}, u32[]{:S(2)}) copy-start(s32[128]{0:T(128)S(1)} %get-tuple-element.4) | copy-start | bytes 1540
  265.9 1.4 copy-start.1
  267.3 1.4 copy-start.3
  293.2 41.2 %all-to-all-start.3 = ((bf16[128,2,512]{2,1,0:T(2,128)(2,1)}), bf16[128,2,512]{2,1,0:T(2,128)(2,1)S(1)}, u32[]{:S(2)}, u32[]{:S(2)}) async-start(bf16[128,2,512]{2,1,0:T(2,128)(2,1)} %all_to_all.41), calls=%async_computation.5 | async-start | bytes 524288 | tf_op jit(solution)/shard_map/all_to_all | solution.py:35
Sparse Core Ops, SparseCore 0:
  104.6 22.0 reduce-scatter.2
  270.6 20.7 reduce-scatter.4
where the time goes:
time: 344 us; the launch traced here: 343 us
  blocking collectives  178 us (52%)
  waiting for transfers between devices  87.1 us (25%)
  starting transfers between devices  37.2 us (11%)
  between operations  14.3 us (4%)
  local copies, waits for them, and re-layouts  13.8 us (4%)
  matrix products  9.94 us (3%)
    all_to_all x2, blocking collectives, to_experts(): lax.all_to_all(buckets, 'expert', split_axis=0, concat_axis=0, tiled=True)  146 us
    all_to_all x2, waiting for transfers between devices, to_homes(): lax.all_to_all(summed, 'expert', split_axis=0, concat_axis=0, tiled=True)  44 us
    reduce_scatter x2, waiting for transfers between devices, to_homes(): lax.psum_scatter(partial_value.astype(jnp.bfloat16), 'half', scatter_dime...  43.1 us
    all_to_all x2, starting transfers between devices, to_homes(): lax.all_to_all(summed, 'expert', split_axis=0, concat_axis=0, tiled=True)  37.1 us
    all_gather x2, blocking collectives, to_experts(): whole = lax.all_gather(items, 'half', axis=1, tiled=True)  20.5 us
    psum x1, blocking collectives, shards(): gram = lax.psum(gram_part, 'half')  11.8 us
  transfers between devices with their start and end apart: 4, of which 4 were waited for; matrix products, arithmetic and copies ran while one was open for 0% of the time, Pallas kernels for 0%

commit v1 on v0

v1 whole, which is shorter than its diff:
```python
import math

import jax
import jax.numpy as jnp
from jax import lax
from jax.experimental import pallas as pl
from jax.experimental.pallas import tpu as pltpu
from jax.sharding import Mesh
from jax.sharding import PartitionSpec as P

orth_weight = 0.25
NY, NZ, NC, NH = 4, 16, 2, 4
TOK, TOPK, WIDE, PART = 16, 8, 2048, 512
PAIRS = TOK * TOPK
ROWS = 256
F32, BF16 = jnp.float32, jnp.bfloat16
HIGHEST = lax.Precision.HIGHEST


def iota(shape, dim):
    return lax.broadcasted_iota(jnp.int32, shape, dim)


def one_hot(where):
    return jnp.where(where, 1.0, 0.0).astype(BF16)


def dot(a, b, dims=((1,), (0,)), precision=None):
    return lax.dot_general(a, b, (dims, ((), ())), precision=precision, preferred_element_type=F32)


def call(body, outs, *operands, vmem=32 << 20):
    specs = [pl.BlockSpec(memory_space=pltpu.SMEM if o.ndim == 1 else pltpu.VMEM) for o in operands]
    return pl.pallas_call(
        body,
        out_shape=[jax.ShapeDtypeStruct(shape, kind) for shape, kind in outs],
        in_specs=specs,
        out_specs=[pl.BlockSpec(memory_space=pltpu.VMEM) for _ in outs],
        compiler_params=pltpu.CompilerParams(vmem_limit_bytes=vmem),
    )(*operands)


def select_body(z_ref, a_ref, out_ref):
    every = a_ref[...].reshape(NZ * TOK, PART + 128)
    named = dot(one_hot(iota((TOPK, 128), 0) == iota((TOPK, 128), 1)), every[:, PART:], ((1,), (1,)))
    row, lane = iota((ROWS, 1), 0), iota((1, ROWS), 1)
    expert = (((row >> 6) * NZ + z_ref[0]) * NC + ((row >> 5) & 1)).astype(F32)
    found = named[0:1, :] == expert
    for k in range(1, TOPK):
        found = found | (named[k : k + 1, :] == expert)
    found = found & (((row >> 1) & 15) == (lane >> 4))
    left, right = iota((ROWS, ROWS), 0), iota((ROWS, ROWS), 1)
    earlier = one_hot(((left >> 4) == (right >> 4)) & (left < right))
    rank = dot(one_hot(found), earlier)
    pick = one_hot(found & (rank == (row & 1).astype(F32)))
    chosen = dot(pick, every[:, :PART]).astype(BF16).reshape(NY * NC, 32, PART)
    for h in range(NH):
        out_ref[:, h] = chosen


def home_body(ids_ref, probs_ref, up_ref, pm_ref, share_ref, su_ref, mask_ref):
    pair, lane = iota((PAIRS, 1), 0), iota((1, PAIRS), 1)
    repeat = one_hot((iota((PAIRS, TOK), 0) >> 3) == iota((PAIRS, TOK), 1))
    ids = ids_ref[...].astype(BF16)
    tall = dot(repeat, ids)
    col = iota((PAIRS, 16), 1)
    ids_col = jnp.sum(jnp.where(col == (pair & 7), tall, 0.0), axis=1, keepdims=True)
    pad_col = jnp.sum(jnp.where(col == 8, tall, 0.0), axis=1, keepdims=True)
    flat = dot(ids, repeat, ((0,), (1,)))
    ids_row = jnp.sum(jnp.where(iota((16, PAIRS), 0) == (lane & 7), flat, 0.0), axis=0, keepdims=True)
    before = (ids_col == ids_row) & ((lane >> 3) < (pair >> 3))
    slot = jnp.sum(jnp.where(before, 1.0, 0.0), axis=1, keepdims=True)
    row = iota((1, ROWS), 1)
    expert = ((((row >> 2) & 3) * NZ + (row >> 4)) * NC + ((row >> 1) & 1)).astype(F32)
    pm_ref[...] = one_hot((expert == ids_col) & ((row & 1).astype(F32) == slot))
    probs = probs_ref[...]
    shares = probs / jnp.sum(probs, axis=1, keepdims=True)
    wide = repeat.astype(F32)
    share_tall = dot(wide, shares, precision=HIGHEST)
    share_col = jnp.sum(jnp.where(iota((PAIRS, TOPK), 1) == (pair & 7), share_tall, 0.0), axis=1, keepdims=True)
    share_flat = dot(shares, wide, ((0,), (1,)), precision=HIGHEST)
    share_row = jnp.sum(jnp.where(iota((TOPK, PAIRS), 0) == (lane & 7), share_flat, 0.0), axis=0, keepdims=True)
    share_ref[...] = jnp.where(iota((TOK, PAIRS), 0) == (iota((TOK, PAIRS), 1) >> 3), share_row, 0.0)
    su_ref[...] = (pad_col * share_col) * dot(repeat, up_ref[...])
    same = ((lane >> 3) == (pair >> 3)) & (lane != pair)
    mask_ref[...] = jnp.where(same, pad_col * (orth_weight / math.sqrt(WIDE)), 0.0)


def forward_body(x_ref, wg_ref, wu_ref, wd_ref, out_ref, dgate_ref, dup_ref):
    gate = up = None
    for h in range(NH):
        x = x_ref[:, h].reshape(ROWS, PART)
        g = dot(x, wg_ref[h * PART : (h + 1) * PART, :])
        u = dot(x, wu_ref[h * PART : (h + 1) * PART, :])
        gate, up = (g, u) if gate is None else (gate + g, up + u)
    sigma = 1.0 / (1.0 + jnp.exp(-gate))
    act = gate * sigma
    hidden = (act * up).astype(BF16)
    for h in range(NH):
        part = dot(hidden, wd_ref[:, h * PART : (h + 1) * PART])
        out_ref[:, h] = part.astype(BF16).reshape(NY * NC, 32, PART)
    dup_ref[...] = act
    dgate_ref[...] = up * sigma * (1.0 + gate * (1.0 - sigma))


def backward_body(g_ref, wg_ref, wu_ref, wd_ref, dgate_ref, dup_ref, out_ref):
    act = None
    for h in range(NH):
        a = dot(g_ref[:, h].reshape(ROWS, PART), wd_ref[:, h * PART : (h + 1) * PART], ((1,), (1,)))
        act = a if act is None else act + a
    gate = (act * dgate_ref[...]).astype(BF16)
    up = (act * dup_ref[...]).astype(BF16)
    for h in range(NH):
        part = dot(gate, wg_ref[h * PART : (h + 1) * PART, :], ((1,), (1,)))
        part = part + dot(up, wu_ref[h * PART : (h + 1) * PART, :], ((1,), (1,)))
        out_ref[:, h] = part.astype(BF16).reshape(NY * NC, 32, PART)


def reduce_body(p_ref, out_ref):
    total = p_ref[:, 0].astype(F32)
    for h in range(1, NH):
        total = total + p_ref[:, h].astype(F32)
    row, lane = iota((ROWS, ROWS), 0), iota((ROWS, ROWS), 1)
    order = one_hot(lane == ((row >> 1) & 7) * 32 + (row >> 4) * 2 + (row & 1))
    moved = dot(order, total.astype(BF16).reshape(ROWS, PART)).astype(BF16)
    out_ref[...] = moved.reshape(NZ, 16, PART)


def spread_body(r_ref, out_ref):
    row, lane = iota((ROWS, ROWS), 0), iota((ROWS, ROWS), 1)
    order = one_hot(lane == ((row >> 1) & 15) * 16 + (row >> 5) * 2 + (row & 1))
    moved = dot(order, r_ref[...].reshape(ROWS, PART)).astype(BF16).reshape(NY * NC, 32, PART)
    for h in range(NH):
        out_ref[:, h] = moved


def gram_body(r_ref, pm_ref, share_ref, out_ref, gram_ref, layer_ref):
    out = dot(pm_ref[...], r_ref[...].reshape(ROWS, PART)).astype(BF16)
    full = dot(out, out, ((1,), (1,)))
    full = jnp.where((iota((PAIRS, PAIRS), 0) >> 3) == (iota((PAIRS, PAIRS), 1) >> 3), full, 0.0)
    packed = jnp.sum(full.reshape(TOK, TOPK, PAIRS), axis=0)
    for h in range(NH):
        gram_ref[h] = packed
    out_ref[...] = out
    layer_ref[...] = dot(share_ref[...], out.astype(F32), precision=HIGHEST).astype(BF16)


def grad_body(gram_ref, out_ref, su_ref, mask_ref, pm_ref, rows_ref):
    packed = (gram_ref[0] + gram_ref[1]) + (gram_ref[2] + gram_ref[3])
    full = jnp.broadcast_to(packed[None], (TOK, TOPK, PAIRS)).reshape(PAIRS, PAIRS)
    grad = su_ref[...] + dot(full * mask_ref[...], out_ref[...].astype(F32), precision=HIGHEST)
    rows = dot(pm_ref[...], grad.astype(BF16), ((0,), (0,))).astype(BF16)
    rows_ref[...] = rows.reshape(NZ, 16, PART)


def combine_body(r_ref, pm_ref, out_ref):
    repeat = one_hot(iota((TOK, PAIRS), 0) == (iota((TOK, PAIRS), 1) >> 3))
    pick = dot(repeat, pm_ref[...]).astype(BF16)
    out_ref[...] = dot(pick, r_ref[...].reshape(ROWS, PART)).astype(BF16)


def over_z(x):
    return lax.all_to_all(x, "z", 0, 0, tiled=True)


def over_plane(x):
    shape = x.shape
    x = lax.all_to_all(x.reshape(NY * NC * NH, 32, PART), ("y", "c", "h"), 0, 0, tiled=True)
    return x.reshape(shape)


def shards(tokens, upstream, expert_ids, gate_probs, pad_mask, gate_weight, up_weight, down_weight):
    wg, wu, wd = gate_weight[0], up_weight[0], down_weight[0]
    tagged = jnp.concatenate([tokens, jnp.pad(expert_ids.astype(BF16), ((0, 0), (0, 128 - TOPK)))], axis=1)
    every = over_z(jnp.broadcast_to(tagged[None], (NZ, TOK, PART + 128)))
    packed_ids = jnp.concatenate([expert_ids, pad_mask[:, None], jnp.zeros((TOK, 7), jnp.int32)], axis=1).astype(F32)
    pm, share, su, mask = call(
        home_body,
        [((PAIRS, ROWS), BF16), ((TOK, PAIRS), F32), ((PAIRS, PART), F32), ((PAIRS, PAIRS), F32)],
        packed_ids, gate_probs, upstream,
    )
    plane = ((NY * NC, NH, 32, PART), BF16)
    ring = ((NZ, 16, PART), BF16)
    hidden = ((ROWS, wg.shape[1]), F32)
    (picked,) = call(select_body, [plane], lax.axis_index("z").astype(jnp.int32).reshape(1), every)
    rows_in = over_plane(picked)
    partial, dgate, dup = call(forward_body, [plane, hidden, hidden], rows_in, wg, wu, wd)
    (summed,) = call(reduce_body, [ring], over_plane(partial))
    out, gram, layer_out = call(
        gram_body,
        [((PAIRS, PART), BF16), ((NH, TOPK, PAIRS), F32), ((TOK, PART), BF16)],
        over_z(summed), pm, share,
    )
    gram = lax.all_to_all(gram, "h", 0, 0, tiled=True)
    (grad_rows,) = call(grad_body, [ring], gram, out, su, mask, pm)
    (spread,) = call(spread_body, [plane], over_z(grad_rows))
    (partial,) = call(backward_body, [plane], over_plane(spread), wg, wu, wd, dgate, dup)
    (summed,) = call(reduce_body, [ring], over_plane(partial))
    (grad_tokens,) = call(combine_body, [((TOK, PART), BF16)], over_z(summed), pm)
    return (layer_out, grad_tokens)


def solution(mesh):
    fine = Mesh(mesh.devices.reshape(NY, NZ, NC, NH), ("y", "z", "c", "h"))
    expert = ("y", "z", "c")
    in_specs = (
        P(expert, "h"),
        P(expert, "h"),
        P(expert, None),
        P(expert, None),
        P(expert),
        P(expert, None, "h"),
        P(expert, None, "h"),
        P(expert, "h", None),
    )
    return jax.shard_map(shards, mesh=fine, in_specs=in_specs, out_specs=(P(expert, "h"), P(expert, "h")), check_vma=False)
```

time: 344 us -> 218 us (0.63)
  the two profiles are of different devices: /device:TPU:1 before, /device:TPU:64 now
where the time goes in v1:
time: 218 us
  blocking collectives  142 us (65%)
  waiting for transfers between devices  36.7 us (17%)
  starting transfers between devices  21 us (10%)
  Pallas kernels  8.98 us (4%)
  local copies, waits for them, and re-layouts  6.47 us (3%)
    all_to_all x4, blocking collectives, over_plane(): lax.all_to_all(x.reshape(NY * NC * NH, 32, PART), ('y', 'c', 'h'), 0, 0,...  87.8 us
    all_to_all x2, blocking collectives, over_z(): return lax.all_to_all(x, 'z', 0, 0, tiled=True)  46.8 us
    all_to_all x2, waiting for transfers between devices, over_z(): return lax.all_to_all(x, 'z', 0, 0, tiled=True)  36.7 us
    all_to_all x2, starting transfers between devices, over_z(): return lax.all_to_all(x, 'z', 0, 0, tiled=True)  21 us
    pallas_call x10, Pallas kernels, call(): pl.pallas_call(body, out_shape=[jax.ShapeDtypeStruct(shape, kind) for sha...  8.98 us
    all_to_all x1, blocking collectives, shards(): gram = lax.all_to_all(gram, 'h', 0, 0, tiled=True)  7.73 us
    unnamed x31, local copies, waits for them, and re-layouts  5.55 us
  transfers between devices with their start and end apart: 2, of which 2 were waited for; matrix products, arithmetic and copies ran while one was open for 0% of the time, Pallas kernels for 0%

profile of v1, /device:TPU:64, one launch (start us, length us, event | category | flops | bytes accessed | tf_op | source)
XLA Modules:
  0.0 217.7 jit_solution(10985976628538892424)
XLA Ops:
  0.6 0.7 convert_element_type.8
  1.3 0.1 copy.14
  1.4 0.7 fusion.1
  2.1 0.8 broadcast_in_dim.12
  2.9 14.8 %all-to-all-start = ((bf16[16,16,640]{2,1,0:T(8,128)(2,1)}), bf16[16,16,640]{2,1,0:T(8,128)(2,1)S(1)}, u32[]{:S(2)}, u32[]{:S(2)}) async-start(bf16[16,16,640]{2,1,0:T(8,128)(2,1)} %broadcast_in_dim.12), calls=%async_computation | async-start | bytes 655360 | tf_op jit(solution)/shard_map/all_to_all | solution.py:163
  17.7 20.7 %all-to-all-done.a_ref = bf16[16,16,640]{2,1,0:T(8,128)(2,1)S(1)} async-done(((bf16[16,16,640]{2,1,0:T(8,128)(2,1)}), bf16[16,16,640]{2,1,0:T(8,128)(2,1)S(1)}, u32[]{:S(2)}, u32[]{:S(2)}) %all-to-all-start) | async-done | bytes 327712 | tf_op jit(solution)/shard_map/all_to_all | solution.py:163
  38.4 0.7 shard_map.95
  39.1 24.3 %all_to_all.45 = bf16[32,32,512]{2,1,0:T(8,128)(2,1)S(1)} all-to-all(bf16[32,32,512]{2,1,0:T(8,128)(2,1)S(1)} %bitcast.22), channel_id=1, replica_groups=mesh['y'=4,'z'=16,'c'=2,'h'=4] {'y','c','h'}, dimensions={0} | all-to-all | bytes 2097152 | tf_op jit(solution)/shard_map/all_to_all | solution.py:168
  63.4 1.4 copy-done.2
  64.8 1.9 shard_map.96
  66.7 0.7 copy-done.4
  67.4 0.7 copy-done.6
  68.2 21.2 %all_to_all.46 = bf16[32,32,512]{2,1,0:T(8,128)(2,1)S(1)} all-to-all(bf16[32,32,512]{2,1,0:T(8,128)(2,1)S(1)} %bitcast.26), channel_id=1, replica_groups=mesh['y'=4,'z'=16,'c'=2,'h'=4] {'y','c','h'}, dimensions={0} | all-to-all | bytes 2097152 | tf_op jit(solution)/shard_map/all_to_all | solution.py:168
  89.4 1.0 shard_map.97
  90.4 6.2 %all-to-all-start.3 = ((bf16[16,16,512]{2,1,0:T(8,128)(2,1)}), bf16[16,16,512]{2,1,0:T(8,128)(2,1)S(1)}, u32[]{:S(2)}, u32[]{:S(2)}) async-start(bf16[16,16,512]{2,1,0:T(8,128)(2,1)} %shard_map.97), calls=%async_computation.3 | async-start | bytes 524288 | tf_op jit(solution)/shard_map/all_to_all | solution.py:163
  96.7 0.1 copy.12
  97.1 0.7 copy-done.10
  97.8 0.4 shard_map.98
  98.2 0.7 copy-done.8
  98.9 16.0 %all-to-all-done.3.r_ref = bf16[16,16,512]{2,1,0:T(8,128)(2,1)S(1)} async-done(((bf16[16,16,512]{2,1,0:T(8,128)(2,1)}), bf16[16,16,512]{2,1,0:T(8,128)(2,1)S(1)}, u32[]{:S(2)}, u32[]{:S(2)}) %all-to-all-start.3) | async-done | bytes 262176 | tf_op jit(solution)/shard_map/all_to_all | solution.py:163
  114.9 1.1 shard_map.99
  115.9 7.7 %all_to_all.47.gram_ref = f32[4,8,128]{2,1,0:T(8,128)S(1)} all-to-all(f32[4,8,128]{2,1,0:T(8,128)S(1)} %get-tuple-element.16), channel_id=1, replica_groups=mesh['y'=4,'z'=16,'c'=2,'h'=4] {'h'}, dimensions={0} | all-to-all | bytes 32768 | tf_op jit(solution)/shard_map/all_to_all | solution.py:194
  123.7 0.9 copy-done.9
  124.6 0.6 shard_map.100
  125.2 23.0 %all_to_all.48.r_ref = bf16[16,16,512]{2,1,0:T(8,128)(2,1)S(1)} all-to-all(bf16[16,16,512]{2,1,0:T(8,128)(2,1)S(1)} %shard_map.100), channel_id=1, replica_groups=mesh['y'=4,'z'=16,'c'=2,'h'=4] {'z'}, dimensions={0} | all-to-all | bytes 524288 | tf_op jit(solution)/shard_map/all_to_all | solution.py:163
  148.3 0.2 shard_map.101
  148.5 21.3 %all_to_all.49 = bf16[32,32,512]{2,1,0:T(8,128)(2,1)S(1)} all-to-all(bf16[32,32,512]{2,1,0:T(8,128)(2,1)S(1)} %bitcast.20), channel_id=1, replica_groups=mesh['y'=4,'z'=16,'c'=2,'h'=4] {'y','c','h'}, dimensions={0} | all-to-all | bytes 2097152 | tf_op jit(solution)/shard_map/all_to_all | solution.py:168
  169.8 1.9 shard_map.102
  171.7 21.1 %all_to_all.50 = bf16[32,32,512]{2,1,0:T(8,128)(2,1)S(1)} all-to-all(bf16[32,32,512]{2,1,0:T(8,128)(2,1)S(1)} %bitcast.25), channel_id=1, replica_groups=mesh['y'=4,'z'=16,'c'=2,'h'=4] {'y','c','h'}, dimensions={0} | all-to-all | bytes 2097152 | tf_op jit(solution)/shard_map/all_to_all | solution.py:168
  192.8 0.3 shard_map.103
  193.1 23.7 %all_to_all.51.r_ref = bf16[16,16,512]{2,1,0:T(8,128)(2,1)S(1)} all-to-all(bf16[16,16,512]{2,1,0:T(8,128)(2,1)S(1)} %shard_map.103), channel_id=1, replica_groups=mesh['y'=4,'z'=16,'c'=2,'h'=4] {'z'}, dimensions={0} | all-to-all | bytes 524288 | tf_op jit(solution)/shard_map/all_to_all | solution.py:163
  216.8 0.9 shard_map.104
  (27 shorter events, 0.3 us)
Async XLA Ops:
  2.9 35.5 %all-to-all-start = ((bf16[16,16,640]{2,1,0:T(8,128)(2,1)}), bf16[16,16,640]{2,1,0:T(8,128)(2,1)S(1)}, u32[]{:S(2)}, u32[]{:S(2)}) async-start(bf16[16,16,640]{2,1,0:T(8,128)(2,1)} %broadcast_in_dim.12), calls=%async_computation | async-start | bytes 655360 | tf_op jit(solution)/shard_map/all_to_all | solution.py:163
  38.4 25.0 %copy-start = (bf16[1,2048,384]{2,1,0:T(8,128)(2,1)S(1)}, bf16[1,2048,384]{2,1,0:T(8,128)(2,1)}, u32[]{:S(2)}) copy-start(bf16[1,2048,384]{2,1,0:T(8,128)(2,1)} %param.13) | copy-start | bytes 4718596
  38.4 25.0 %copy-start.1 = (bf16[1,2048,384]{2,1,0:T(8,128)(2,1)S(1)}, bf16[1,2048,384]{2,1,0:T(8,128)(2,1)}, u32[]{:S(2)}) copy-start(bf16[1,2048,384]{2,1,0:T(8,128)(2,1)} %param.14) | copy-start | bytes 4718596
  63.4 1.4 copy-start.2
  66.7 0.8 copy-start.4
  67.4 0.7 copy-start.6
  68.2 28.5 %copy-start.11 = (s32[16,8]{0,1:T(8,128)S(1)}, s32[16,8]{0,1:T(8,128)}, u32[]{:S(2)}) copy-start(s32[16,8]{0,1:T(8,128)} %param.10) | copy-start | bytes 1540
  68.2 28.6 %copy-start.13 = (s32[16]{0:T(128)S(1)}, s32[16]{0:T(128)}, u32[]{:S(2)}) copy-start(s32[16]{0:T(128)} %param.12) | copy-start | bytes 196
  68.2 28.7 %copy-start.12 = (f32[16,8]{0,1:T(8,128)S(1)}, f32[16,8]{0,1:T(8,128)}, u32[]{:S(2)}) copy-start(f32[16,8]{0,1:T(8,128)} %param.11) | copy-start | bytes 1540
  90.4 24.5 %all-to-all-start.3 = ((bf16[16,16,512]{2,1,0:T(8,128)(2,1)}), bf16[16,16,512]{2,1,0:T(8,128)(2,1)S(1)}, u32[]{:S(2)}, u32[]{:S(2)}) async-start(bf16[16,16,512]{2,1,0:T(8,128)(2,1)} %shard_map.97), calls=%async_computation.3 | async-start | bytes 524288 | tf_op jit(solution)/shard_map/all_to_all | solution.py:163
  97.1 0.7 copy-start.10
  98.2 0.7 copy-start.8
  123.7 1.0 copy-start.9
  148.3 21.5 %copy-start.3 = (bf16[1,384,2048]{2,1,0:T(8,128)(2,1)S(1)}, bf16[1,384,2048]{2,1,0:T(8,128)(2,1)}, u32[]{:S(2)}) copy-start(bf16[1,384,2048]{2,1,0:T(8,128)(2,1)} %param.15) | copy-start | bytes 4718596
  148.3 21.5 %copy-start.5 = (f32[256,384]{1,0:T(8,128)S(1)}, f32[256,384]{1,0:T(8,128)}, u32[]{:S(2)}) copy-start(f32[256,384]{1,0:T(8,128)} %copy-done.4) | copy-start | bytes 1179652
  148.3 21.5 %copy-start.7 = (f32[256,384]{1,0:T(8,128)S(1)}, f32[256,384]{1,0:T(8,128)}, u32[]{:S(2)}) copy-start(f32[256,384]{1,0:T(8,128)} %copy-done.6) | copy-start | bytes 1179652

commit v2 on v1

v2 whole, which is shorter than its diff:
```python
import math

import jax
import jax.numpy as jnp
from jax import lax
from jax.experimental import pallas as pl
from jax.experimental.pallas import tpu as pltpu
from jax.sharding import Mesh
from jax.sharding import PartitionSpec as P

orth_weight = 0.25
NY, NZ, NC, NH = 4, 16, 2, 4
TOK, TOPK, WIDE, PART = 16, 8, 2048, 512
PAIRS = TOK * TOPK
ROWS, HALF = 256, 128
F32, BF16 = jnp.float32, jnp.bfloat16
HIGHEST = lax.Precision.HIGHEST


def iota(shape, dim):
    return lax.broadcasted_iota(jnp.int32, shape, dim)


def one_hot(where):
    return jnp.where(where, 1.0, 0.0).astype(BF16)


def dot(a, b, dims=((1,), (0,)), precision=None):
    return lax.dot_general(a, b, (dims, ((), ())), precision=precision, preferred_element_type=F32)


def call(body, outs, *operands, vmem=8 << 20, space=None, remote=(), scratch=(), cost=None):
    specs = [pl.BlockSpec(memory_space=pltpu.SMEM if o.ndim == 1 else pltpu.VMEM) for o in operands]
    specs += [pl.BlockSpec(memory_space=pltpu.HBM) for _ in remote]
    return pl.pallas_call(
        body,
        out_shape=[(space or jax.ShapeDtypeStruct)(shape, kind) for shape, kind in outs],
        in_specs=specs,
        out_specs=[pl.BlockSpec(memory_space=pltpu.VMEM) for _ in outs],
        scratch_shapes=scratch,
        cost_estimate=cost,
        compiler_params=pltpu.CompilerParams(vmem_limit_bytes=vmem),
    )(*operands, *(pltpu.with_memory_space_constraint(r, pltpu.HBM) for r in remote))


def fetch(pairs, sems):
    copies = [pltpu.make_async_copy(src, dst, sems.at[i]) for i, (src, dst) in enumerate(pairs)]
    for c in copies:
        c.start()
    for c in copies:
        c.wait()


def pack_body(tok_hbm, ids_hbm, out_ref, tok_ref, ids_ref, sems):
    fetch([(tok_hbm, tok_ref), (ids_hbm, ids_ref)], sems)
    place = one_hot(iota((TOPK, 128), 0) == iota((TOPK, 128), 1))
    ids = dot(ids_ref[...].astype(F32).astype(BF16), place, ((0,), (0,))).astype(BF16)
    row = jnp.concatenate([tok_ref[...], ids], axis=1)
    for z in range(NZ):
        out_ref[z] = row


def select_body(where_ref, a_ref, out_ref):
    every = a_ref[...].reshape(NZ * TOK, PART + 128)
    named = dot(one_hot(iota((TOPK, 128), 0) == iota((TOPK, 128), 1)), every[:, PART:], ((1,), (1,)))
    row, lane = iota((ROWS, 1), 0), iota((1, ROWS), 1)
    expert = (((row >> 6) * NZ + where_ref[0]) * NC + (((row >> 5) + where_ref[1]) & 1)).astype(F32)
    found = named[0:1, :] == expert
    for k in range(1, TOPK):
        found = found | (named[k : k + 1, :] == expert)
    found = found & (((row >> 1) & 15) == (lane >> 4))
    left, right = iota((ROWS, ROWS), 0), iota((ROWS, ROWS), 1)
    earlier = one_hot(((left >> 4) == (right >> 4)) & (left < right))
    rank = dot(one_hot(found), earlier)
    pick = one_hot(found & (rank == (row & 1).astype(F32)))
    chosen = dot(pick, every[:, :PART]).astype(BF16).reshape(NY, 64, PART)
    for h in range(NH):
        out_ref[:, h] = chosen


def home_body(where_ref, ids_ref, probs_ref, pad_ref, up_ref, pm_ref, share_ref, su_ref, mask_ref):
    pair, lane = iota((PAIRS, 1), 0), iota((1, PAIRS), 1)
    owner = (iota((PAIRS, TOK), 0) >> 3) == iota((PAIRS, TOK), 1)
    repeat = one_hot(owner)
    ids = ids_ref[...].astype(F32).astype(BF16)
    tall = dot(repeat, ids, ((1,), (1,)))
    mine = iota((PAIRS, TOPK), 1) == (pair & 7)
    ids_col = jnp.sum(jnp.where(mine, tall, 0.0), axis=1, keepdims=True)
    pad_col = jnp.sum(jnp.where(owner, pad_ref[...].astype(F32), 0.0), axis=1, keepdims=True)
    flat = dot(ids, repeat, ((1,), (1,)))
    mine_row = iota((TOPK, PAIRS), 0) == (lane & 7)
    ids_row = jnp.sum(jnp.where(mine_row, flat, 0.0), axis=0, keepdims=True)
    before = (ids_col == ids_row) & ((lane >> 3) < (pair >> 3))
    slot = jnp.sum(jnp.where(before, 1.0, 0.0), axis=1, keepdims=True)
    row = iota((1, ROWS), 1)
    expert = ((((row >> 2) & 3) * NZ + (row >> 4)) * NC + (((row >> 1) + where_ref[1]) & 1)).astype(F32)
    pm_ref[...] = one_hot((expert == ids_col) & ((row & 1).astype(F32) == slot))
    probs = probs_ref[...]
    shares = probs / jnp.sum(probs, axis=0, keepdims=True)
    wide = repeat.astype(F32)
    share_tall = dot(wide, shares, ((1,), (1,)), HIGHEST)
    share_col = jnp.sum(jnp.where(mine, share_tall, 0.0), axis=1, keepdims=True)
    share_flat = dot(shares, wide, ((1,), (1,)), HIGHEST)
    share_row = jnp.sum(jnp.where(mine_row, share_flat, 0.0), axis=0, keepdims=True)
    share_ref[...] = jnp.where(iota((TOK, PAIRS), 0) == (iota((TOK, PAIRS), 1) >> 3), share_row, 0.0)
    su_ref[...] = (pad_col * share_col) * dot(repeat, up_ref[...])
    same = ((lane >> 3) == (pair >> 3)) & (lane != pair)
    mask_ref[...] = jnp.where(same, pad_col * (orth_weight / math.sqrt(WIDE)), 0.0)


def forward_body(x_ref, wg_ref, wu_ref, *refs):
    hbm, (out_ref, dgate_ref, dup_ref), held, sems = refs[:4], refs[4:7], refs[7:11], refs[11]
    copies = [pltpu.make_async_copy(src, dst, sems.at[i]) for i, (src, dst) in enumerate(zip(hbm, held))]
    for c in copies:
        c.start()
    for b, (hg, hu, hd) in enumerate(((wg_ref, wu_ref, held[0]), held[1:])):
        if b:
            copies[1].wait()
            copies[2].wait()
        gate = up = None
        for h in range(NH):
            x = x_ref[:, h, b * 32 : b * 32 + 32].reshape(HALF, PART)
            g = dot(x, hg[h * PART : (h + 1) * PART, :])
            u = dot(x, hu[h * PART : (h + 1) * PART, :])
            gate, up = (g, u) if gate is None else (gate + g, up + u)
        sigma = 1.0 / (1.0 + jnp.exp(-gate))
        act = gate * sigma
        hidden = (act * up).astype(BF16)
        dup_ref[b] = act
        dgate_ref[b] = up * sigma * (1.0 + gate * (1.0 - sigma))
        copies[3 if b else 0].wait()
        for h in range(NH):
            part = dot(hidden, hd[:, h * PART : (h + 1) * PART])
            out_ref[:, h, b * 32 : b * 32 + 32] = part.astype(BF16).reshape(NY, 32, PART)


def backward_body(g_ref, dgate_ref, dup_ref, wg_ref, wu_ref, wd_ref, *refs):
    hbm, out_ref, held, sems = refs[:3], refs[3], refs[4:7], refs[7]
    copies = [pltpu.make_async_copy(src, dst, sems.at[i]) for i, (src, dst) in enumerate(zip(hbm, held))]
    for c in (copies[2], copies[0], copies[1]):
        c.start()
    for b, (hg, hu, hd) in enumerate(((wg_ref, wu_ref, wd_ref), held)):
        if b:
            for c in copies:
                c.wait()
        act = None
        for h in range(NH):
            g = g_ref[:, h, b * 32 : b * 32 + 32].reshape(HALF, PART)
            a = dot(g, hd[:, h * PART : (h + 1) * PART], ((1,), (1,)))
            act = a if act is None else act + a
        gate = (act * dgate_ref[b]).astype(BF16)
        up = (act * dup_ref[b]).astype(BF16)
        for h in range(NH):
            part = dot(gate, hg[h * PART : (h + 1) * PART, :], ((1,), (1,)))
            part = part + dot(up, hu[h * PART : (h + 1) * PART, :], ((1,), (1,)))
            out_ref[:, h, b * 32 : b * 32 + 32] = part.astype(BF16).reshape(NY, 32, PART)


def reduce_body(p_ref, out_ref):
    total = p_ref[:, 0].astype(F32)
    for h in range(1, NH):
        total = total + p_ref[:, h].astype(F32)
    row, lane = iota((ROWS, ROWS), 0), iota((ROWS, ROWS), 1)
    order = one_hot(lane == ((row >> 1) & 7) * 32 + (row >> 4) * 2 + (row & 1))
    moved = dot(order, total.astype(BF16).reshape(ROWS, PART)).astype(BF16)
    out_ref[...] = moved.reshape(NZ, 16, PART)


def spread_body(r_ref, out_ref):
    row, lane = iota((ROWS, ROWS), 0), iota((ROWS, ROWS), 1)
    order = one_hot(lane == ((row >> 1) & 15) * 16 + (row >> 5) * 2 + (row & 1))
    moved = dot(order, r_ref[...].reshape(ROWS, PART)).astype(BF16).reshape(NY, 64, PART)
    for h in range(NH):
        out_ref[:, h] = moved


def gram_body(r_ref, pm_ref, share_ref, out_ref, gram_ref, layer_ref):
    out = dot(pm_ref[...], r_ref[...].reshape(ROWS, PART)).astype(BF16)
    full = dot(out, out, ((1,), (1,)))
    full = jnp.where((iota((PAIRS, PAIRS), 0) >> 3) == (iota((PAIRS, PAIRS), 1) >> 3), full, 0.0)
    packed = jnp.sum(full.reshape(TOK, TOPK, PAIRS), axis=0)
    for h in range(NH):
        gram_ref[h] = packed
    out_ref[...] = out
    layer_ref[...] = dot(share_ref[...], out.astype(F32), precision=HIGHEST).astype(BF16)


def grad_body(gram_ref, out_ref, su_ref, mask_ref, pm_ref, rows_ref):
    packed = (gram_ref[0] + gram_ref[1]) + (gram_ref[2] + gram_ref[3])
    full = jnp.broadcast_to(packed[None], (TOK, TOPK, PAIRS)).reshape(PAIRS, PAIRS)
    grad = su_ref[...] + dot(full * mask_ref[...], out_ref[...].astype(F32), precision=HIGHEST)
    rows = dot(pm_ref[...], grad.astype(BF16), ((0,), (0,))).astype(BF16)
    rows_ref[...] = rows.reshape(NZ, 16, PART)


def combine_body(r_ref, pm_ref, out_ref):
    repeat = one_hot(iota((TOK, PAIRS), 0) == (iota((TOK, PAIRS), 1) >> 3))
    pick = dot(repeat, pm_ref[...]).astype(BF16)
    out_ref[...] = dot(pick, r_ref[...].reshape(ROWS, PART)).astype(BF16)


def over_z(x):
    return lax.all_to_all(x, "z", 0, 0, tiled=True)


def over_plane(x):
    shape = x.shape
    return lax.all_to_all(x.reshape(NY * NH, 64, PART), ("y", "h"), 0, 0, tiled=True).reshape(shape)


def shards(tokens, upstream, expert_ids, gate_probs, pad_mask, gate_weight, up_weight, down_weight):
    own = [gate_weight[0], up_weight[0], down_weight[0]]
    plane = ((NY, NH, 64, PART), BF16)
    ring = ((NZ, 16, PART), BF16)
    hidden = ((2, HALF, own[0].shape[1]), F32)
    ids, probs = expert_ids.T, gate_probs.T
    where = jnp.stack([lax.axis_index("z"), lax.axis_index("c")]).astype(jnp.int32)
    (tagged,) = call(
        pack_body, [((NZ, TOK, PART + 128), BF16)], remote=(tokens, ids), space=pltpu.HBM,
        scratch=[pltpu.VMEM((TOK, PART), BF16), pltpu.VMEM((TOPK, TOK), jnp.int32), pltpu.SemaphoreType.DMA((2,))],
    )
    every = over_z(tagged)
    known = call(
        home_body,
        [((PAIRS, ROWS), BF16), ((TOK, PAIRS), F32), ((PAIRS, PART), F32), ((PAIRS, PAIRS), F32)],
        where, ids, probs, pad_mask.reshape(1, TOK), upstream, space=pltpu.VMEM,
    )
    swapped = [lax.ppermute(w, "c", [(0, 1), (1, 0)]) for w in own]
    every, known = lax.optimization_barrier((every, known))
    pm, share, su, mask = known
    (picked,) = call(select_body, [plane], where, every, space=pltpu.HBM)
    rows_in = over_plane(picked)
    held = [pltpu.VMEM(w.shape, BF16) for w in swapped]
    partial, dgate, dup = call(
        forward_body, [plane, hidden, hidden], rows_in, own[0], own[1], remote=(own[2], *swapped), space=pltpu.VMEM,
        vmem=24 << 20, scratch=[held[2], *held, pltpu.SemaphoreType.DMA((4,))],
    )
    (summed,) = call(reduce_body, [ring], over_plane(partial))
    out, gram, layer_out = call(
        gram_body,
        [((PAIRS, PART), BF16), ((NH, TOPK, PAIRS), F32), ((TOK, PART), BF16)],
        over_z(summed), pm, share,
    )
    gram = lax.all_to_all(gram, "h", 0, 0, tiled=True)
    (grad_rows,) = call(grad_body, [ring], gram, out, su, mask, pm)
    (spread,) = call(spread_body, [plane], over_z(grad_rows))
    (partial,) = call(
        backward_body, [plane], over_plane(spread), dgate, dup, *own, remote=swapped,
        vmem=24 << 20, scratch=[*held, pltpu.SemaphoreType.DMA((3,))],
    )
    (summed,) = call(reduce_body, [ring], over_plane(partial))
    (grad_tokens,) = call(combine_body, [((TOK, PART), BF16)], over_z(summed), pm)
    return (layer_out, grad_tokens)


def solution(mesh):
    fine = Mesh(mesh.devices.reshape(NY, NZ, NC, NH), ("y", "z", "c", "h"))
    expert = ("y", "z", "c")
    in_specs = (
        P(expert, "h"),
        P(expert, "h"),
        P(expert, None),
        P(expert, None),
        P(expert),
        P(expert, None, "h"),
        P(expert, None, "h"),
        P(expert, "h", None),
    )
    return jax.shard_map(shards, mesh=fine, in_specs=in_specs, out_specs=(P(expert, "h"), P(expert, "h")), check_vma=False)
```

time: 218 us -> 206 us (0.945)
  the two profiles are of different devices: /device:TPU:64 before, /device:TPU:32 now
where the time goes in v2:
time: 206 us; the launch traced here: 205 us
  blocking collectives  128 us (62%)
  starting transfers between devices  28.6 us (14%)
  waiting for transfers between devices  25.1 us (12%)
  Pallas kernels  18.2 us (9%)
  local copies, waits for them, and re-layouts  4.1 us (2%)
    all_to_all x3, blocking collectives, over_z(): return lax.all_to_all(x, 'z', 0, 0, tiled=True)  68.4 us
    all_to_all x3, blocking collectives, over_plane(): lax.all_to_all(x.reshape(NY * NH, 64, PART), ('y', 'h'), 0, 0, tiled=True)  51.9 us
    pallas_call x11, Pallas kernels, call(): pl.pallas_call(body, out_shape=[(space or jax.ShapeDtypeStruct)(shape, ki...  18.2 us
    all_to_all x1, waiting for transfers between devices, over_plane(): lax.all_to_all(x.reshape(NY * NH, 64, PART), ('y', 'h'), 0, 0, tiled=True)  16.4 us
    all_to_all x1, starting transfers between devices, over_z(): return lax.all_to_all(x, 'z', 0, 0, tiled=True)  15.2 us
    all_to_all x1, waiting for transfers between devices, over_z(): return lax.all_to_all(x, 'z', 0, 0, tiled=True)  8.66 us
    all_to_all x1, blocking collectives, shards(): gram = lax.all_to_all(gram, 'h', 0, 0, tiled=True)  7.7 us
    all_to_all x1, starting transfers between devices, over_plane(): lax.all_to_all(x.reshape(NY * NH, 64, PART), ('y', 'h'), 0, 0, tiled=True)  7.08 us
  transfers between devices with their start and end apart: 5, of which 2 were waited for; matrix products, arithmetic and copies ran while one was open for 0% of the time, Pallas kernels for 2%

profile of v2, /device:TPU:32, one launch (start us, length us, event | category | flops | bytes accessed | tf_op | source)
XLA Modules:
  0.0 204.8 jit_solution(1273776276204578733)
XLA Ops:
  0.6 1.6 shard_map.95
  2.3 15.2 %all-to-all-start = ((bf16[16,16,640]{2,1,0:T(8,128)(2,1)}), bf16[16,16,640]{2,1,0:T(8,128)(2,1)S(1)}, u32[]{:S(2)}, u32[]{:S(2)}) async-start(bf16[16,16,640]{2,1,0:T(8,128)(2,1)} %shard_map.95), calls=%async_computation | async-start | bytes 655360 | tf_op jit(solution)/shard_map/all_to_all | solution.py:203
  17.5 1.9 collective-permute-start
  19.4 2.4 %collective-permute-start.1 = (bf16[2048,384]{1,0:T(8,128)(2,1)}, bf16[2048,384]{1,0:T(8,128)(2,1)}, u32[]{:S(2)}, u32[]{:S(2)}) collective-permute-start(bf16[2048,384]{1,0:T(8,128)(2,1)} %bitcast.19), channel_id=1, source_target_pairs={{0,4},{4,0},{1,5},{5,1},{2,6},{6,2},{3,7},{7,3},{8,12},{12,8},{9,1... | collective-permute-start | bytes 4718600 | tf_op jit(solution)/shard_map/ppermute | solution.py:228
  21.8 1.9 collective-permute-start.2
  23.8 0.1 pad_add_fusion.where_ref
  23.9 0.7 copy-done.7
  24.5 0.7 copy-done.8
  25.3 0.7 copy-done.9
  25.9 0.7 copy-done.10
  26.6 0.9 shard_map.96
  27.5 0.7 copy-done.3
  28.2 0.6 copy-done.5
  28.8 8.7 %all-to-all-done.a_ref = bf16[16,16,640]{2,1,0:T(8,128)(2,1)S(1)} async-done(((bf16[16,16,640]{2,1,0:T(8,128)(2,1)}), bf16[16,16,640]{2,1,0:T(8,128)(2,1)S(1)}, u32[]{:S(2)}, u32[]{:S(2)}) %all-to-all-start) | async-done | bytes 327712 | tf_op jit(solution)/shard_map/all_to_all | solution.py:203
  37.5 2.2 %shard_map.97 = bf16[4,4,64,512]{3,2,1,0:T(8,128)(2,1)} custom-call(s32[2]{0:T(128)S(1)} %pad_add_fusion.where_ref, bf16[16,16,640]{2,1,0:T(8,128)(2,1)S(1)} %all-to-all-done.a_ref), custom_call_target="tpu_custom_call" | custom-call | tf_op jit(solution)/shard_map/pallas_call | solution.py:35
  39.7 7.1 %all-to-all-start.1 = ((bf16[16,64,512]{2,1,0:T(8,128)(2,1)}), bf16[16,64,512]{2,1,0:T(8,128)(2,1)}, u32[]{:S(2)}, u32[]{:S(2)}) async-start(bf16[16,64,512]{2,1,0:T(8,128)(2,1)} %bitcast.35), calls=%async_computation.1 | async-start | bytes 2097152 | tf_op jit(solution)/shard_map/all_to_all | solution.py:208
  46.8 16.4 %all-to-all-done.1 = bf16[16,64,512]{2,1,0:T(8,128)(2,1)} async-done(((bf16[16,64,512]{2,1,0:T(8,128)(2,1)}), bf16[16,64,512]{2,1,0:T(8,128)(2,1)}, u32[]{:S(2)}, u32[]{:S(2)}) %all-to-all-start.1) | async-done | bytes 1048608 | tf_op jit(solution)/shard_map/all_to_all | solution.py:208
  63.3 4.8 %shard_map.98 = (bf16[4,4,64,512]{3,2,1,0:T(8,128)(2,1)S(1)}, f32[2,128,384]{2,1,0:T(8,128)S(1)}, f32[2,128,384]{2,1,0:T(8,128)S(1)}) custom-call(bf16[4,4,64,512]{3,2,1,0:T(8,128)(2,1)} %bitcast.6.x_ref, bf16[2048,384]{1,0:T(8,128)(2,1)S(1)} %bitcast.17, bf16[2048,384]{1,0:T(8,128)(2,1)S(1)} %bitcast.20, bf16[384,2048]{1,0:T(8,128)(2,1)} %bitcast.23, ...), custom_call_target="tpu_custom_call" | custom-call | tf_op jit(solution)/shard_map/pallas_call | solution.py:35
  68.1 19.7 %all_to_all.45 = bf16[16,64,512]{2,1,0:T(8,128)(2,1)S(1)} all-to-all(bf16[16,64,512]{2,1,0:T(8,128)(2,1)S(1)} %bitcast.30), channel_id=1, replica_groups=mesh['y'=4,'z'=16,'c'=2,'h'=4] {'y','h'}, dimensions={0} | all-to-all | bytes 2097152 | tf_op jit(solution)/shard_map/all_to_all | solution.py:208
  87.8 0.3 shard_map.99
  88.1 25.2 %all_to_all.46.r_ref = bf16[16,16,512]{2,1,0:T(8,128)(2,1)S(1)} all-to-all(bf16[16,16,512]{2,1,0:T(8,128)(2,1)S(1)} %shard_map.99), channel_id=1, replica_groups=mesh['y'=4,'z'=16,'c'=2,'h'=4] {'z'}, dimensions={0} | all-to-all | bytes 524288 | tf_op jit(solution)/shard_map/all_to_all | solution.py:203
  113.3 1.1 shard_map.100
  114.4 7.7 %all_to_all.47.gram_ref = f32[4,8,128]{2,1,0:T(8,128)S(1)} all-to-all(f32[4,8,128]{2,1,0:T(8,128)S(1)} %get-tuple-element.26), channel_id=1, replica_groups=mesh['y'=4,'z'=16,'c'=2,'h'=4] {'h'}, dimensions={0} | all-to-all | bytes 32768 | tf_op jit(solution)/shard_map/all_to_all | solution.py:244
  122.1 0.6 shard_map.101
  122.7 20.6 %all_to_all.48.r_ref = bf16[16,16,512]{2,1,0:T(8,128)(2,1)S(1)} all-to-all(bf16[16,16,512]{2,1,0:T(8,128)(2,1)S(1)} %shard_map.101), channel_id=1, replica_groups=mesh['y'=4,'z'=16,'c'=2,'h'=4] {'z'}, dimensions={0} | all-to-all | bytes 524288 | tf_op jit(solution)/shard_map/all_to_all | solution.py:203
  143.2 0.2 shard_map.102
  143.5 16.4 %all_to_all.49 = bf16[16,64,512]{2,1,0:T(8,128)(2,1)S(1)} all-to-all(bf16[16,64,512]{2,1,0:T(8,128)(2,1)S(1)} %bitcast.28), channel_id=1, replica_groups=mesh['y'=4,'z'=16,'c'=2,'h'=4] {'y','h'}, dimensions={0} | all-to-all | bytes 2097152 | tf_op jit(solution)/shard_map/all_to_all | solution.py:208
  159.9 5.3 %shard_map.103 = bf16[4,4,64,512]{3,2,1,0:T(8,128)(2,1)S(1)} custom-call(bf16[4,4,64,512]{3,2,1,0:T(8,128)(2,1)S(1)} %bitcast.25, f32[2,128,384]{2,1,0:T(8,128)S(1)} %get-tuple-element.30.dgate_ref, f32[2,128,384]{2,1,0:T(8,128)S(1)} %get-tuple-element.31.dup_ref, bf16[2048,384]{1,0:T(8,128)(2,1)S(1)} %bitcast.18, bf16[2048,384]{1,0:T(8,128)(2,1)S(1)} %bitcast.21, ...), custom_call_target="tpu_custom_call" | custom-call | tf_op jit(solution)/shard_map/pallas_call | solution.py:35
  165.2 15.8 %all_to_all.50 = bf16[16,64,512]{2,1,0:T(8,128)(2,1)S(1)} all-to-all(bf16[16,64,512]{2,1,0:T(8,128)(2,1)S(1)} %bitcast.26), channel_id=1, replica_groups=mesh['y'=4,'z'=16,'c'=2,'h'=4] {'y','h'}, dimensions={0} | all-to-all | bytes 2097152 | tf_op jit(solution)/shard_map/all_to_all | solution.py:208
  181.0 0.3 shard_map.104
  181.3 22.6 %all_to_all.51.r_ref = bf16[16,16,512]{2,1,0:T(8,128)(2,1)S(1)} all-to-all(bf16[16,16,512]{2,1,0:T(8,128)(2,1)S(1)} %shard_map.104), channel_id=1, replica_groups=mesh['y'=4,'z'=16,'c'=2,'h'=4] {'z'}, dimensions={0} | all-to-all | bytes 524288 | tf_op jit(solution)/shard_map/all_to_all | solution.py:203
  203.9 0.9 shard_map.105
  (19 shorter events, 0.0 us)
Async XLA Ops:
  2.3 35.2 %all-to-all-start = ((bf16[16,16,640]{2,1,0:T(8,128)(2,1)}), bf16[16,16,640]{2,1,0:T(8,128)(2,1)S(1)}, u32[]{:S(2)}, u32[]{:S(2)}) async-start(bf16[16,16,640]{2,1,0:T(8,128)(2,1)} %shard_map.95), calls=%async_computation | async-start | bytes 655360 | tf_op jit(solution)/shard_map/all_to_all | solution.py:203
  17.5 29.3 %collective-permute-start = (bf16[2048,384]{1,0:T(8,128)(2,1)}, bf16[2048,384]{1,0:T(8,128)(2,1)}, u32[]{:S(2)}, u32[]{:S(2)}) collective-permute-start(bf16[2048,384]{1,0:T(8,128)(2,1)} %bitcast.16), channel_id=1, source_target_pairs={{0,4},{4,0},{1,5},{5,1},{2,6},{6,2},{3,7},{7,3},{8,12},{12,8},{9,1... | collective-permute-start | bytes 4718600 | tf_op jit(solution)/shard_map/ppermute | solution.py:228
  19.4 27.4 %collective-permute-start.1 = (bf16[2048,384]{1,0:T(8,128)(2,1)}, bf16[2048,384]{1,0:T(8,128)(2,1)}, u32[]{:S(2)}, u32[]{:S(2)}) collective-permute-start(bf16[2048,384]{1,0:T(8,128)(2,1)} %bitcast.19), channel_id=1, source_target_pairs={{0,4},{4,0},{1,5},{5,1},{2,6},{6,2},{3,7},{7,3},{8,12},{12,8},{9,1... | collective-permute-start | bytes 4718600 | tf_op jit(solution)/shard_map/ppermute | solution.py:228
  21.8 25.0 %collective-permute-start.2 = (bf16[384,2048]{1,0:T(8,128)(2,1)}, bf16[384,2048]{1,0:T(8,128)(2,1)}, u32[]{:S(2)}, u32[]{:S(2)}) collective-permute-start(bf16[384,2048]{1,0:T(8,128)(2,1)} %bitcast.22), channel_id=1, source_target_pairs={{0,4},{4,0},{1,5},{5,1},{2,6},{6,2},{3,7},{7,3},{8,12},{12,8},{9,1... | collective-permute-start | bytes 4718600 | tf_op jit(solution)/shard_map/ppermute | solution.py:228
  23.9 0.7 copy-start.7
  24.5 0.7 copy-start.8
  25.3 0.7 copy-start.9
  25.9 0.7 copy-start.10
  27.5 0.7 copy-start.3
  28.2 0.6 copy-start.5
  37.5 25.8 %copy-start = (bf16[1,2048,384]{2,1,0:T(8,128)(2,1)S(1)}, bf16[1,2048,384]{2,1,0:T(8,128)(2,1)}, u32[]{:S(2)}) copy-start(bf16[1,2048,384]{2,1,0:T(8,128)(2,1)} %param.13) | copy-start | bytes 4718596
  37.5 25.8 %copy-start.1 = (bf16[1,2048,384]{2,1,0:T(8,128)(2,1)S(1)}, bf16[1,2048,384]{2,1,0:T(8,128)(2,1)}, u32[]{:S(2)}) copy-start(bf16[1,2048,384]{2,1,0:T(8,128)(2,1)} %param.14) | copy-start | bytes 4718596
  39.7 23.6 %all-to-all-start.1 = ((bf16[16,64,512]{2,1,0:T(8,128)(2,1)}), bf16[16,64,512]{2,1,0:T(8,128)(2,1)}, u32[]{:S(2)}, u32[]{:S(2)}) async-start(bf16[16,64,512]{2,1,0:T(8,128)(2,1)} %bitcast.35), calls=%async_computation.1 | async-start | bytes 2097152 | tf_op jit(solution)/shard_map/all_to_all | solution.py:208
  87.8 34.3 %copy-start.4 = (f32[128,512]{1,0:T(8,128)S(1)}, f32[128,512]{1,0:T(8,128)}, u32[]{:S(2)}) copy-start(f32[128,512]{1,0:T(8,128)} %copy-done.3) | copy-start | bytes 786436
  87.8 34.3 %copy-start.6 = (f32[128,128]{1,0:T(8,128)S(1)}, f32[128,128]{1,0:T(8,128)}, u32[]{:S(2)}) copy-start(f32[128,128]{1,0:T(8,128)} %copy-done.5) | copy-start | bytes 196612
  143.2 16.7 %copy-start.2 = (bf16[1,384,2048]{2,1,0:T(8,128)(2,1)S(1)}, bf16[1,384,2048]{2,1,0:T(8,128)(2,1)}, u32[]{:S(2)}) copy-start(bf16[1,384,2048]{2,1,0:T(8,128)(2,1)} %param.15) | copy-start | bytes 4718596

commit v3 on v2

v3 whole, which is shorter than its diff:
```python
import math

import jax
import jax.numpy as jnp
from jax import lax
from jax.experimental import pallas as pl
from jax.experimental.pallas import tpu as pltpu
from jax.sharding import Mesh
from jax.sharding import PartitionSpec as P

orth_weight = 0.25
NY, NZ, NC, NH = 4, 16, 2, 4
TOK, TOPK, WIDE, PART = 16, 8, 2048, 512
PAIRS = TOK * TOPK
ROWS, HALF = 256, 128
F32, BF16 = jnp.float32, jnp.bfloat16
HIGHEST = lax.Precision.HIGHEST


def iota(shape, dim):
    return lax.broadcasted_iota(jnp.int32, shape, dim)


def one_hot(where):
    return jnp.where(where, 1.0, 0.0).astype(BF16)


def dot(a, b, dims=((1,), (0,)), precision=None):
    return lax.dot_general(a, b, (dims, ((), ())), precision=precision, preferred_element_type=F32)


def call(body, outs, *operands, vmem=8 << 20, spaces=None, remote=(), scratch=()):
    specs = [pl.BlockSpec(memory_space=pltpu.SMEM if o.ndim == 1 else pltpu.VMEM) for o in operands]
    specs += [pl.BlockSpec(memory_space=pltpu.HBM) for _ in remote]
    return pl.pallas_call(
        body,
        out_shape=[make(*out) for make, out in zip(spaces or [jax.ShapeDtypeStruct] * len(outs), outs)],
        in_specs=specs,
        out_specs=[pl.BlockSpec(memory_space=pltpu.VMEM) for _ in outs],
        scratch_shapes=scratch,
        compiler_params=pltpu.CompilerParams(vmem_limit_bytes=vmem),
    )(*operands, *(pltpu.with_memory_space_constraint(r, pltpu.HBM) for r in remote))


def owners():
    return (iota((PAIRS, TOK), 0) >> 3) == iota((PAIRS, TOK), 1)


def place_body(tok_hbm, ids_hbm, out_ref, pm_ref, tok_ref, ids_ref, sems):
    copies = [pltpu.make_async_copy(ids_hbm, ids_ref, sems.at[0]), pltpu.make_async_copy(tok_hbm, tok_ref, sems.at[1])]
    for c in copies:
        c.start()
    pair, lane = iota((PAIRS, 1), 0), iota((1, PAIRS), 1)
    repeat = one_hot(owners())
    copies[0].wait()
    ids = ids_ref[...].astype(F32).astype(BF16)
    tall = dot(repeat, ids, ((1,), (1,)))
    ids_col = jnp.sum(jnp.where(iota((PAIRS, TOPK), 1) == (pair & 7), tall, 0.0), axis=1, keepdims=True)
    flat = dot(ids, repeat, ((1,), (1,)))
    ids_row = jnp.sum(jnp.where(iota((TOPK, PAIRS), 0) == (lane & 7), flat, 0.0), axis=0, keepdims=True)
    before = (ids_col == ids_row) & ((lane >> 3) < (pair >> 3))
    slot = jnp.sum(jnp.where(before, 1.0, 0.0), axis=1, keepdims=True)
    row = iota((1, ROWS), 1)
    other = ((row >> 1) + lax.axis_index("c")) & 1
    expert = ((((row >> 2) & 3) * NZ + (row >> 4)) * NC + other).astype(F32)
    pm = one_hot((expert == ids_col) & ((row & 1).astype(F32) == slot))
    pm_ref[...] = pm
    pick = dot(pm, repeat, ((0,), (0,))).astype(BF16)
    copies[1].wait()
    out_ref[...] = dot(pick, tok_ref[...]).astype(BF16).reshape(NZ, 16, PART)


def home_body(probs_ref, pad_ref, up_ref, share_ref, su_ref, mask_ref):
    pair, lane = iota((PAIRS, 1), 0), iota((1, PAIRS), 1)
    owner = owners()
    repeat = one_hot(owner)
    pad_col = jnp.sum(jnp.where(owner, pad_ref[...].astype(F32), 0.0), axis=1, keepdims=True)
    probs = probs_ref[...]
    shares = probs / jnp.sum(probs, axis=0, keepdims=True)
    wide = repeat.astype(F32)
    share_tall = dot(wide, shares, ((1,), (1,)), HIGHEST)
    mine = iota((PAIRS, TOPK), 1) == (pair & 7)
    share_col = jnp.sum(jnp.where(mine, share_tall, 0.0), axis=1, keepdims=True)
    share_flat = dot(shares, wide, ((1,), (1,)), HIGHEST)
    share_row = jnp.sum(jnp.where(iota((TOPK, PAIRS), 0) == (lane & 7), share_flat, 0.0), axis=0, keepdims=True)
    share_ref[...] = jnp.where(iota((TOK, PAIRS), 0) == (iota((TOK, PAIRS), 1) >> 3), share_row, 0.0)
    su_ref[...] = (pad_col * share_col) * dot(repeat, up_ref[...])
    same = ((lane >> 3) == (pair >> 3)) & (lane != pair)
    mask_ref[...] = jnp.where(same, pad_col * (orth_weight / math.sqrt(WIDE)), 0.0)


def wide_rows(ref, b):
    return jnp.concatenate([ref[:, h, b * 32 : b * 32 + 32].reshape(HALF, PART) for h in range(NH)], axis=1)


def put_rows(ref, b, rows):
    for h in range(NH):
        ref[:, h, b * 32 : b * 32 + 32] = rows[:, h * PART : (h + 1) * PART].reshape(NY, 32, PART)


def forward_body(x_ref, wg_ref, wu_ref, *refs):
    hbm, (out_ref, dgate_ref, dup_ref), held, sems = refs[:4], refs[4:7], refs[7:11], refs[11]
    copies = [pltpu.make_async_copy(src, dst, sems.at[i]) for i, (src, dst) in enumerate(zip(hbm, held))]
    for c in copies:
        c.start()
    for b, (hg, hu, hd) in enumerate(((wg_ref, wu_ref, held[0]), held[1:])):
        if b:
            copies[1].wait()
            copies[2].wait()
        x = wide_rows(x_ref, b)
        gate, up = dot(x, hg[...]), dot(x, hu[...])
        sigma = 1.0 / (1.0 + jnp.exp(-gate))
        act = gate * sigma
        hidden = (act * up).astype(BF16)
        dup_ref[b] = act
        dgate_ref[b] = up * sigma * (1.0 + gate * (1.0 - sigma))
        copies[3 if b else 0].wait()
        put_rows(out_ref, b, dot(hidden, hd[...]).astype(BF16))


def backward_body(g_ref, dgate_ref, dup_ref, *refs):
    out_ref = refs[6]
    for b, (hg, hu, hd) in enumerate((refs[0:3], refs[3:6])):
        act = dot(wide_rows(g_ref, b), hd[...], ((1,), (1,)))
        gate, up = (act * dgate_ref[b]).astype(BF16), (act * dup_ref[b]).astype(BF16)
        rows = dot(gate, hg[...], ((1,), (1,))) + dot(up, hu[...], ((1,), (1,)))
        put_rows(out_ref, b, rows.astype(BF16))


def reduce_body(p_ref, out_ref):
    total = p_ref[:, 0].astype(F32)
    for h in range(1, NH):
        total = total + p_ref[:, h].astype(F32)
    row, lane = iota((ROWS, ROWS), 0), iota((ROWS, ROWS), 1)
    order = one_hot(lane == ((row >> 1) & 7) * 32 + (row >> 4) * 2 + (row & 1))
    moved = dot(order, total.astype(BF16).reshape(ROWS, PART)).astype(BF16)
    out_ref[...] = moved.reshape(NZ, 16, PART)


def spread_body(r_ref, out_ref):
    row, lane = iota((ROWS, ROWS), 0), iota((ROWS, ROWS), 1)
    order = one_hot(lane == ((row >> 1) & 15) * 16 + (row >> 5) * 2 + (row & 1))
    moved = dot(order, r_ref[...].reshape(ROWS, PART)).astype(BF16).reshape(NY, 64, PART)
    for h in range(NH):
        out_ref[:, h] = moved


def gram_body(r_ref, pm_ref, share_ref, out_ref, gram_ref, layer_ref):
    out = dot(pm_ref[...], r_ref[...].reshape(ROWS, PART)).astype(BF16)
    full = dot(out, out, ((1,), (1,)))
    full = jnp.where((iota((PAIRS, PAIRS), 0) >> 3) == (iota((PAIRS, PAIRS), 1) >> 3), full, 0.0)
    packed = jnp.sum(full.reshape(TOK, TOPK, PAIRS), axis=0)
    for h in range(NH):
        gram_ref[h] = packed
    out_ref[...] = out
    layer_ref[...] = dot(share_ref[...], out.astype(F32), precision=HIGHEST).astype(BF16)


def grad_body(gram_ref, out_ref, su_ref, mask_ref, pm_ref, rows_ref):
    packed = (gram_ref[0] + gram_ref[1]) + (gram_ref[2] + gram_ref[3])
    full = jnp.broadcast_to(packed[None], (TOK, TOPK, PAIRS)).reshape(PAIRS, PAIRS)
    grad = su_ref[...] + dot(full * mask_ref[...], out_ref[...].astype(F32), precision=HIGHEST)
    rows = dot(pm_ref[...], grad.astype(BF16), ((0,), (0,))).astype(BF16)
    rows_ref[...] = rows.reshape(NZ, 16, PART)


def combine_body(r_ref, pm_ref, out_ref):
    repeat = one_hot(iota((TOK, PAIRS), 0) == (iota((TOK, PAIRS), 1) >> 3))
    pick = dot(repeat, pm_ref[...]).astype(BF16)
    out_ref[...] = dot(pick, r_ref[...].reshape(ROWS, PART)).astype(BF16)


def over_z(x):
    return lax.all_to_all(x, "z", 0, 0, tiled=True)


def over_plane(x):
    shape = x.shape
    return lax.all_to_all(x.reshape(NY * NH, 64, PART), ("y", "h"), 0, 0, tiled=True).reshape(shape)


def shards(tokens, upstream, expert_ids, gate_probs, pad_mask, gate_weight, up_weight, down_weight):
    own = [gate_weight[0], up_weight[0], down_weight[0]]
    plane = ((NY, NH, 64, PART), BF16)
    ring = ((NZ, 16, PART), BF16)
    hidden = ((2, HALF, own[0].shape[1]), F32)
    placed, pm = call(
        place_body, [ring, ((PAIRS, ROWS), BF16)], remote=(tokens, expert_ids.T), spaces=(pltpu.HBM, pltpu.VMEM),
        scratch=[pltpu.VMEM((TOK, PART), BF16), pltpu.VMEM((TOPK, TOK), jnp.int32), pltpu.SemaphoreType.DMA((2,))],
    )
    rows = over_z(placed)
    swapped = [lax.ppermute(w, "c", [(0, 1), (1, 0)]) for w in own]
    known = call(
        home_body,
        [((TOK, PAIRS), F32), ((PAIRS, PART), F32), ((PAIRS, PAIRS), F32)],
        gate_probs.T, pad_mask.reshape(1, TOK), upstream, spaces=(pltpu.VMEM,) * 3,
    )
    rows, (share, su, mask) = lax.optimization_barrier((rows, known))
    (spread,) = call(spread_body, [plane], rows, spaces=(pltpu.HBM,))
    rows_in = over_plane(spread)
    late = [own[2], *swapped]
    partial, dgate, dup, *late = call(
        forward_body, [plane, hidden, hidden, *((w.shape, BF16) for w in late)], rows_in, own[0], own[1],
        remote=late, spaces=(pltpu.VMEM,) * 7, vmem=24 << 20, scratch=[pltpu.SemaphoreType.DMA((4,))],
    )
    (summed,) = call(reduce_body, [ring], over_plane(partial))
    out, gram, layer_out = call(
        gram_body,
        [((PAIRS, PART), BF16), ((NH, TOPK, PAIRS), F32), ((TOK, PART), BF16)],
        over_z(summed), pm, share,
    )
    gram = lax.all_to_all(gram, "h", 0, 0, tiled=True)
    (grad_rows,) = call(grad_body, [ring], gram, out, su, mask, pm)
    (spread,) = call(spread_body, [plane], over_z(grad_rows))
    (partial,) = call(
        backward_body, [plane], over_plane(spread), dgate, dup, own[0], own[1], *late, vmem=24 << 20,
    )
    (summed,) = call(reduce_body, [ring], over_plane(partial))
    (grad_tokens,) = call(combine_body, [((TOK, PART), BF16)], over_z(summed), pm)
    return (layer_out, grad_tokens)


def solution(mesh):
    fine = Mesh(mesh.devices.reshape(NY, NZ, NC, NH), ("y", "z", "c", "h"))
    expert = ("y", "z", "c")
    in_specs = (
        P(expert, "h"),
        P(expert, "h"),
        P(expert, None),
        P(expert, None),
        P(expert),
        P(expert, None, "h"),
        P(expert, None, "h"),
        P(expert, "h", None),
    )
    return jax.shard_map(shards, mesh=fine, in_specs=in_specs, out_specs=(P(expert, "h"), P(expert, "h")), check_vma=False)
```

time: 206 us -> 200 us (0.971)
  Pallas kernels: 18.2 us -> 15.1 us
    pallas_call x11, Pallas kernels: 18.2 us -> 15.1 us  [call(): pl.pallas_call(body, out_shape=[make(*out) for make, out in zip(spaces or...]
  transfers between devices with their start and end apart: 5 -> 5, of which waited for: 2 -> 2; matrix products, arithmetic and copies ran while one was open for 0% -> 0% of each run, Pallas kernels for 2% -> 1%
where the time goes in v3:
time: 200 us
  blocking collectives  127 us (64%)
  starting transfers between devices  28.6 us (14%)
  waiting for transfers between devices  25.1 us (13%)
  Pallas kernels  15.1 us (8%)
  local copies, waits for them, and re-layouts  2.78 us (1%)
    all_to_all x3, blocking collectives, over_z(): return lax.all_to_all(x, 'z', 0, 0, tiled=True)  67.5 us
    all_to_all x3, blocking collectives, over_plane(): lax.all_to_all(x.reshape(NY * NH, 64, PART), ('y', 'h'), 0, 0, tiled=True)  52 us
    all_to_all x1, waiting for transfers between devices, over_plane(): lax.all_to_all(x.reshape(NY * NH, 64, PART), ('y', 'h'), 0, 0, tiled=True)  16.5 us
    all_to_all x1, starting transfers between devices, over_z(): return lax.all_to_all(x, 'z', 0, 0, tiled=True)  15.2 us
    pallas_call x11, Pallas kernels, call(): pl.pallas_call(body, out_shape=[make(*out) for make, out in zip(spaces or...  15.1 us
    all_to_all x1, waiting for transfers between devices, over_z(): return lax.all_to_all(x, 'z', 0, 0, tiled=True)  8.55 us
    all_to_all x1, blocking collectives, shards(): gram = lax.all_to_all(gram, 'h', 0, 0, tiled=True)  7.7 us
    all_to_all x1, starting transfers between devices, over_plane(): lax.all_to_all(x.reshape(NY * NH, 64, PART), ('y', 'h'), 0, 0, tiled=True)  7.19 us
  transfers between devices with their start and end apart: 5, of which 2 were waited for; matrix products, arithmetic and copies ran while one was open for 0% of the time, Pallas kernels for 1%

profile of v3, /device:TPU:32, one launch (start us, length us, event | category | flops | bytes accessed | tf_op | source)
XLA Modules:
  0.0 199.5 jit_solution(6071533130264592519)
XLA Ops:
  0.6 2.1 %shard_map.95 = (bf16[16,16,512]{2,1,0:T(8,128)(2,1)}, bf16[128,256]{1,0:T(8,128)(2,1)S(1)}) custom-call(bf16[16,512]{1,0:T(8,128)(2,1)} %tok_hbm.1, s32[8,16]{1,0:T(8,128)} %bitcast.31), custom_call_target="tpu_custom_call" | custom-call | tf_op jit(solution)/shard_map/pallas_call | solution.py:35
  2.7 15.2 %all-to-all-start = ((bf16[16,16,512]{2,1,0:T(8,128)(2,1)}), bf16[16,16,512]{2,1,0:T(8,128)(2,1)S(1)}, u32[]{:S(2)}, u32[]{:S(2)}) async-start(bf16[16,16,512]{2,1,0:T(8,128)(2,1)} %get-tuple-element.21), calls=%async_computation | async-start | bytes 524288 | tf_op jit(solution)/shard_map/all_to_all | solution.py:174
  18.0 1.9 collective-permute-start
  19.9 2.4 %collective-permute-start.1 = (bf16[2048,384]{1,0:T(8,128)(2,1)}, bf16[2048,384]{1,0:T(8,128)(2,1)}, u32[]{:S(2)}, u32[]{:S(2)}) collective-permute-start(bf16[2048,384]{1,0:T(8,128)(2,1)} %bitcast.17), channel_id=1, source_target_pairs={{0,4},{4,0},{1,5},{5,1},{2,6},{6,2},{3,7},{7,3},{8,12},{12,8},{9,1... | collective-permute-start | bytes 4718600 | tf_op jit(solution)/shard_map/ppermute | solution.py:192
  22.3 1.9 collective-permute-start.2
  24.2 0.0 copy-start.4
  24.2 0.7 copy-done.4
  24.9 0.7 copy-done.5
  25.6 0.7 copy-done.6
  26.3 0.3 shard_map.96
  26.6 0.7 copy-done.2
  27.3 8.6 %all-to-all-done.r_ref = bf16[16,16,512]{2,1,0:T(8,128)(2,1)S(1)} async-done(((bf16[16,16,512]{2,1,0:T(8,128)(2,1)}), bf16[16,16,512]{2,1,0:T(8,128)(2,1)S(1)}, u32[]{:S(2)}, u32[]{:S(2)}) %all-to-all-start) | async-done | bytes 262176 | tf_op jit(solution)/shard_map/all_to_all | solution.py:174
  35.9 1.2 shard_map.97
  37.1 7.2 %all-to-all-start.1 = ((bf16[16,64,512]{2,1,0:T(8,128)(2,1)}), bf16[16,64,512]{2,1,0:T(8,128)(2,1)}, u32[]{:S(2)}, u32[]{:S(2)}) async-start(bf16[16,64,512]{2,1,0:T(8,128)(2,1)} %bitcast.28), calls=%async_computation.1 | async-start | bytes 2097152 | tf_op jit(solution)/shard_map/all_to_all | solution.py:179
  44.3 0.0 collective-permute-done.refs_1_
  44.3 0.0 collective-permute-done.1.refs_2_
  44.3 16.5 %all-to-all-done.1 = bf16[16,64,512]{2,1,0:T(8,128)(2,1)} async-done(((bf16[16,64,512]{2,1,0:T(8,128)(2,1)}), bf16[16,64,512]{2,1,0:T(8,128)(2,1)}, u32[]{:S(2)}, u32[]{:S(2)}) %all-to-all-start.1) | async-done | bytes 1048608 | tf_op jit(solution)/shard_map/all_to_all | solution.py:179
  60.9 4.8 %shard_map.98 = (bf16[4,4,64,512]{3,2,1,0:T(8,128)(2,1)S(1)}, f32[2,128,384]{2,1,0:T(8,128)S(1)}, f32[2,128,384]{2,1,0:T(8,128)S(1)}, bf16[384,2048]{1,0:T(8,128...) custom-call(bf16[4,4,64,512]{3,2,1,0:T(8,128)(2,1)} %bitcast.4.x_ref, ...), custom_call_target="tpu_custom_call" | custom-call | tf_op jit(solution)/shard_map/pallas_call | solution.py:35
  65.7 19.9 %all_to_all.45 = bf16[16,64,512]{2,1,0:T(8,128)(2,1)S(1)} all-to-all(bf16[16,64,512]{2,1,0:T(8,128)(2,1)S(1)} %bitcast.25), channel_id=1, replica_groups=mesh['y'=4,'z'=16,'c'=2,'h'=4] {'y','h'}, dimensions={0} | all-to-all | bytes 2097152 | tf_op jit(solution)/shard_map/all_to_all | solution.py:179
  85.5 0.3 shard_map.99
  85.9 24.4 %all_to_all.46.r_ref = bf16[16,16,512]{2,1,0:T(8,128)(2,1)S(1)} all-to-all(bf16[16,16,512]{2,1,0:T(8,128)(2,1)S(1)} %shard_map.99), channel_id=1, replica_groups=mesh['y'=4,'z'=16,'c'=2,'h'=4] {'z'}, dimensions={0} | all-to-all | bytes 524288 | tf_op jit(solution)/shard_map/all_to_all | solution.py:174
  110.3 1.1 shard_map.100
  111.3 7.7 %all_to_all.47.gram_ref = f32[4,8,128]{2,1,0:T(8,128)S(1)} all-to-all(f32[4,8,128]{2,1,0:T(8,128)S(1)} %get-tuple-element.30), channel_id=1, replica_groups=mesh['y'=4,'z'=16,'c'=2,'h'=4] {'h'}, dimensions={0} | all-to-all | bytes 32768 | tf_op jit(solution)/shard_map/all_to_all | solution.py:212
  119.0 0.6 shard_map.101
  119.6 20.6 %all_to_all.48.r_ref = bf16[16,16,512]{2,1,0:T(8,128)(2,1)S(1)} all-to-all(bf16[16,16,512]{2,1,0:T(8,128)(2,1)S(1)} %shard_map.101), channel_id=1, replica_groups=mesh['y'=4,'z'=16,'c'=2,'h'=4] {'z'}, dimensions={0} | all-to-all | bytes 524288 | tf_op jit(solution)/shard_map/all_to_all | solution.py:174
  140.2 0.2 shard_map.102
  140.4 16.3 %all_to_all.49 = bf16[16,64,512]{2,1,0:T(8,128)(2,1)S(1)} all-to-all(bf16[16,64,512]{2,1,0:T(8,128)(2,1)S(1)} %bitcast.23), channel_id=1, replica_groups=mesh['y'=4,'z'=16,'c'=2,'h'=4] {'y','h'}, dimensions={0} | all-to-all | bytes 2097152 | tf_op jit(solution)/shard_map/all_to_all | solution.py:179
  156.7 3.3 %shard_map.103 = bf16[4,4,64,512]{3,2,1,0:T(8,128)(2,1)S(1)} custom-call(bf16[4,4,64,512]{3,2,1,0:T(8,128)(2,1)S(1)} %bitcast.20, f32[2,128,384]{2,1,0:T(8,128)S(1)} %get-tuple-element.34.dgate_ref, f32[2,128,384]{2,1,0:T(8,128)S(1)} %get-tuple-element.35.dup_ref, bf16[2048,384]{1,0:T(8,128)(2,1)S(1)} %bitcast.16, bf16[2048,384]{1,0:T(8,128)(2,1)S(1)} %bitcast.19, ...), custom_call_target="tpu_custom_call" | custom-call | tf_op jit(solution)/shard_map/pallas_call | solution.py:35
  160.0 15.8 %all_to_all.50 = bf16[16,64,512]{2,1,0:T(8,128)(2,1)S(1)} all-to-all(bf16[16,64,512]{2,1,0:T(8,128)(2,1)S(1)} %bitcast.21), channel_id=1, replica_groups=mesh['y'=4,'z'=16,'c'=2,'h'=4] {'y','h'}, dimensions={0} | all-to-all | bytes 2097152 | tf_op jit(solution)/shard_map/all_to_all | solution.py:179
  175.8 0.3 shard_map.104
  176.2 22.5 %all_to_all.51.r_ref = bf16[16,16,512]{2,1,0:T(8,128)(2,1)S(1)} all-to-all(bf16[16,16,512]{2,1,0:T(8,128)(2,1)S(1)} %shard_map.104), channel_id=1, replica_groups=mesh['y'=4,'z'=16,'c'=2,'h'=4] {'z'}, dimensions={0} | all-to-all | bytes 524288 | tf_op jit(solution)/shard_map/all_to_all | solution.py:174
  198.7 0.9 shard_map.105
  (10 shorter events, 0.0 us)
Async XLA Ops:
  2.7 33.1 %all-to-all-start = ((bf16[16,16,512]{2,1,0:T(8,128)(2,1)}), bf16[16,16,512]{2,1,0:T(8,128)(2,1)S(1)}, u32[]{:S(2)}, u32[]{:S(2)}) async-start(bf16[16,16,512]{2,1,0:T(8,128)(2,1)} %get-tuple-element.21), calls=%async_computation | async-start | bytes 524288 | tf_op jit(solution)/shard_map/all_to_all | solution.py:174
  18.0 26.3 %collective-permute-start = (bf16[2048,384]{1,0:T(8,128)(2,1)}, bf16[2048,384]{1,0:T(8,128)(2,1)}, u32[]{:S(2)}, u32[]{:S(2)}) collective-permute-start(bf16[2048,384]{1,0:T(8,128)(2,1)} %bitcast.14), channel_id=1, source_target_pairs={{0,4},{4,0},{1,5},{5,1},{2,6},{6,2},{3,7},{7,3},{8,12},{12,8},{9,1... | collective-permute-start | bytes 4718600 | tf_op jit(solution)/shard_map/ppermute | solution.py:192
  19.9 24.4 %collective-permute-start.1 = (bf16[2048,384]{1,0:T(8,128)(2,1)}, bf16[2048,384]{1,0:T(8,128)(2,1)}, u32[]{:S(2)}, u32[]{:S(2)}) collective-permute-start(bf16[2048,384]{1,0:T(8,128)(2,1)} %bitcast.17), channel_id=1, source_target_pairs={{0,4},{4,0},{1,5},{5,1},{2,6},{6,2},{3,7},{7,3},{8,12},{12,8},{9,1... | collective-permute-start | bytes 4718600 | tf_op jit(solution)/shard_map/ppermute | solution.py:192
  22.3 22.0 %collective-permute-start.2 = (bf16[384,2048]{1,0:T(8,128)(2,1)}, bf16[384,2048]{1,0:T(8,128)(2,1)}, u32[]{:S(2)}, u32[]{:S(2)}) collective-permute-start(bf16[384,2048]{1,0:T(8,128)(2,1)} %bitcast.29), channel_id=1, source_target_pairs={{0,4},{4,0},{1,5},{5,1},{2,6},{6,2},{3,7},{7,3},{8,12},{12,8},{9,1... | collective-permute-start | bytes 4718600 | tf_op jit(solution)/shard_map/ppermute | solution.py:192
  24.2 0.7 copy-start.4
  24.9 0.7 copy-start.5
  25.6 0.7 copy-start.6
  26.6 0.7 copy-start.2
  35.9 25.0 %copy-start = (bf16[1,2048,384]{2,1,0:T(8,128)(2,1)S(1)}, bf16[1,2048,384]{2,1,0:T(8,128)(2,1)}, u32[]{:S(2)}) copy-start(bf16[1,2048,384]{2,1,0:T(8,128)(2,1)} %param.13) | copy-start | bytes 4718596
  35.9 25.0 %copy-start.1 = (bf16[1,2048,384]{2,1,0:T(8,128)(2,1)S(1)}, bf16[1,2048,384]{2,1,0:T(8,128)(2,1)}, u32[]{:S(2)}) copy-start(bf16[1,2048,384]{2,1,0:T(8,128)(2,1)} %param.14) | copy-start | bytes 4718596
  37.1 23.8 %all-to-all-start.1 = ((bf16[16,64,512]{2,1,0:T(8,128)(2,1)}), bf16[16,64,512]{2,1,0:T(8,128)(2,1)}, u32[]{:S(2)}, u32[]{:S(2)}) async-start(bf16[16,64,512]{2,1,0:T(8,128)(2,1)} %bitcast.28), calls=%async_computation.1 | async-start | bytes 2097152 | tf_op jit(solution)/shard_map/all_to_all | solution.py:179
  85.5 33.5 %copy-start.3 = (f32[128,512]{1,0:T(8,128)S(1)}, f32[128,512]{1,0:T(8,128)}, u32[]{:S(2)}) copy-start(f32[128,512]{1,0:T(8,128)} %copy-done.2) | copy-start | bytes 786436

commit v4 on v3

--- a/solution.py
+++ b/solution.py
@@ -12,7 +12,7 @@
 NY, NZ, NC, NH = 4, 16, 2, 4
 TOK, TOPK, WIDE, PART = 16, 8, 2048, 512
 PAIRS = TOK * TOPK
-ROWS, HALF = 256, 128
+ROWS, HALF, PIECES = 256, 128, 4
 F32, BF16 = jnp.float32, jnp.bfloat16
 HIGHEST = lax.Precision.HIGHEST
 
@@ -27,6 +27,11 @@
 
 def dot(a, b, dims=((1,), (0,)), precision=None):
     return lax.dot_general(a, b, (dims, ((), ())), precision=precision, preferred_element_type=F32)
+
+
+def fine_dot(a, b):
+    high = a.astype(BF16)
+    return dot(high, b) + dot((a - high.astype(F32)).astype(BF16), b)
 
 
 def call(body, outs, *operands, vmem=8 << 20, spaces=None, remote=(), scratch=()):
@@ -36,7 +41,7 @@
         body,
         out_shape=[make(*out) for make, out in zip(spaces or [jax.ShapeDtypeStruct] * len(outs), outs)],
         in_specs=specs,
-        out_specs=[pl.BlockSpec(memory_space=pltpu.VMEM) for _ in outs],
+        out_specs=[pl.BlockSpec(memory_space=pltpu.HBM if body is spread_out_body else pltpu.VMEM) for _ in outs],
         scratch_shapes=scratch,
         compiler_params=pltpu.CompilerParams(vmem_limit_bytes=vmem),
     )(*operands, *(pltpu.with_memory_space_constraint(r, pltpu.HBM) for r in remote))
@@ -98,15 +103,33 @@
         ref[:, h, b * 32 : b * 32 + 32] = rows[:, h * PART : (h + 1) * PART].reshape(NY, 32, PART)
 
 
-def forward_body(x_ref, wg_ref, wu_ref, *refs):
-    hbm, (out_ref, dgate_ref, dup_ref), held, sems = refs[:4], refs[4:7], refs[7:11], refs[11]
-    copies = [pltpu.make_async_copy(src, dst, sems.at[i]) for i, (src, dst) in enumerate(zip(hbm, held))]
+def start(copies):
     for c in copies:
         c.start()
+
+
+def wait(copies):
+    for c in copies:
+        c.wait()
+
+
+def forward_body(wg_ref, wu_ref, x_hbm, *refs):
+    hbm, (out_ref, dgate_ref, dup_ref), held, (x_ref, sems) = refs[:4], refs[4:7], refs[7:11], refs[11:]
+    def parts(i):
+        rows = hbm[i].shape[0] // PIECES
+        return [
+            pltpu.make_async_copy(hbm[i].at[p * rows : (p + 1) * rows], held[i].at[p * rows : (p + 1) * rows], sems.at[i, p])
+            for p in range(PIECES)
+        ]
+
+    copies = [parts(i) for i in range(4)]
+    inputs = [pltpu.make_async_copy(x_hbm.at[:, h], x_ref.at[:, h], sems.at[4, h]) for h in range(NH)]
+    for group in (inputs, *copies):
+        start(group)
+    wait(inputs)
     for b, (hg, hu, hd) in enumerate(((wg_ref, wu_ref, held[0]), held[1:])):
         if b:
-            copies[1].wait()
-            copies[2].wait()
+            wait(copies[1] + copies[2])
         x = wide_rows(x_ref, b)
         gate, up = dot(x, hg[...]), dot(x, hu[...])
         sigma = 1.0 / (1.0 + jnp.exp(-gate))
@@ -114,7 +137,7 @@
         hidden = (act * up).astype(BF16)
         dup_ref[b] = act
         dgate_ref[b] = up * sigma * (1.0 + gate * (1.0 - sigma))
-        copies[3 if b else 0].wait()
+        wait(copies[3 if b else 0])
         put_rows(out_ref, b, dot(hidden, hd[...]).astype(BF16))
 
 
@@ -145,6 +168,17 @@
         out_ref[:, h] = moved
 
 
+def spread_out_body(r_ref, out_hbm, moved_ref, sems):
+    row, lane = iota((ROWS, ROWS), 0), iota((ROWS, ROWS), 1)
+    order = one_hot(lane == ((row >> 1) & 15) * 16 + (row >> 5) * 2 + (row & 1))
+    moved_ref[...] = dot(order, r_ref[...].reshape(ROWS, PART)).astype(BF16).reshape(NY, 64, PART)
+    copies = [pltpu.make_async_copy(moved_ref, out_hbm.at[:, h], sems.at[h]) for h in range(NH)]
+    for c in copies:
+        c.start()
+    for c in copies:
+        c.wait()
+
+
 def gram_body(r_ref, pm_ref, share_ref, out_ref, gram_ref, layer_ref):
     out = dot(pm_ref[...], r_ref[...].reshape(ROWS, PART)).astype(BF16)
     full = dot(out, out, ((1,), (1,)))
@@ -153,13 +187,13 @@
     for h in range(NH):
         gram_ref[h] = packed
     out_ref[...] = out
-    layer_ref[...] = dot(share_ref[...], out.astype(F32), precision=HIGHEST).astype(BF16)
+    layer_ref[...] = fine_dot(share_ref[...], out).astype(BF16)
 
 
 def grad_body(gram_ref, out_ref, su_ref, mask_ref, pm_ref, rows_ref):
     packed = (gram_ref[0] + gram_ref[1]) + (gram_ref[2] + gram_ref[3])
     full = jnp.broadcast_to(packed[None], (TOK, TOPK, PAIRS)).reshape(PAIRS, PAIRS)
-    grad = su_ref[...] + dot(full * mask_ref[...], out_ref[...].astype(F32), precision=HIGHEST)
+    grad = su_ref[...] + fine_dot(full * mask_ref[...], out_ref[...])
     rows = dot(pm_ref[...], grad.astype(BF16), ((0,), (0,))).astype(BF16)
     rows_ref[...] = rows.reshape(NZ, 16, PART)
 
@@ -196,12 +230,15 @@
         gate_probs.T, pad_mask.reshape(1, TOK), upstream, spaces=(pltpu.VMEM,) * 3,
     )
     rows, (share, su, mask) = lax.optimization_barrier((rows, known))
-    (spread,) = call(spread_body, [plane], rows, spaces=(pltpu.HBM,))
+    (spread,) = call(
+        spread_out_body, [plane], rows, spaces=(pltpu.HBM,), scratch=[pltpu.VMEM((NY, 64, PART), BF16), pltpu.SemaphoreType.DMA((NH,))],
+    )
     rows_in = over_plane(spread)
     late = [own[2], *swapped]
     partial, dgate, dup, *late = call(
-        forward_body, [plane, hidden, hidden, *((w.shape, BF16) for w in late)], rows_in, own[0], own[1],
-        remote=late, spaces=(pltpu.VMEM,) * 7, vmem=24 << 20, scratch=[pltpu.SemaphoreType.DMA((4,))],
+        forward_body, [plane, hidden, hidden, *((w.shape, BF16) for w in late)], own[0], own[1],
+        remote=(rows_in, *late), spaces=(pltpu.VMEM,) * 7, vmem=24 << 20,
+        scratch=[pltpu.VMEM(*plane), pltpu.SemaphoreType.DMA((5, NH))],
     )
     (summed,) = call(reduce_body, [ring], over_plane(partial))
     out, gram, layer_out = call(

time: 200 us -> 199 us (level)
  no operation moved by 1% of the time
where the time goes in v4:
time: 199 us; the launch traced here: 198 us
  blocking collectives  127 us (64%)
  starting transfers between devices  28.7 us (14%)
  waiting for transfers between devices  25.1 us (13%)
  Pallas kernels  14 us (7%)
  local copies, waits for them, and re-layouts  2.78 us (1%)
    all_to_all x3, blocking collectives, over_z(): return lax.all_to_all(x, 'z', 0, 0, tiled=True)  67.5 us
    all_to_all x3, blocking collectives, over_plane(): lax.all_to_all(x.reshape(NY * NH, 64, PART), ('y', 'h'), 0, 0, tiled=True)  52 us
    all_to_all x1, waiting for transfers between devices, over_plane(): lax.all_to_all(x.reshape(NY * NH, 64, PART), ('y', 'h'), 0, 0, tiled=True)  16.5 us
    all_to_all x1, starting transfers between devices, over_z(): return lax.all_to_all(x, 'z', 0, 0, tiled=True)  15.2 us
    pallas_call x11, Pallas kernels, call(): pl.pallas_call(body, out_shape=[make(*out) for make, out in zip(spaces or...  14 us
    all_to_all x1, waiting for transfers between devices, over_z(): return lax.all_to_all(x, 'z', 0, 0, tiled=True)  8.55 us
    all_to_all x1, blocking collectives, shards(): gram = lax.all_to_all(gram, 'h', 0, 0, tiled=True)  7.7 us
    all_to_all x1, starting transfers between devices, over_plane(): lax.all_to_all(x.reshape(NY * NH, 64, PART), ('y', 'h'), 0, 0, tiled=True)  7.2 us
  transfers between devices with their start and end apart: 5, of which 2 were waited for; matrix products, arithmetic and copies ran while one was open for 0% of the time, Pallas kernels for 1%

profile of v4, /device:TPU:32, one launch (start us, length us, event | category | flops | bytes accessed | tf_op | source)
XLA Modules:
  0.0 198.5 jit_solution(11517167667610997276)
XLA Ops:
  0.6 2.1 %shard_map.95 = (bf16[16,16,512]{2,1,0:T(8,128)(2,1)}, bf16[128,256]{1,0:T(8,128)(2,1)S(1)}) custom-call(bf16[16,512]{1,0:T(8,128)(2,1)} %tok_hbm.1, s32[8,16]{1,0:T(8,128)} %bitcast.31), custom_call_target="tpu_custom_call" | custom-call | tf_op jit(solution)/shard_map/pallas_call | solution.py:40
  2.7 15.2 %all-to-all-start = ((bf16[16,16,512]{2,1,0:T(8,128)(2,1)}), bf16[16,16,512]{2,1,0:T(8,128)(2,1)S(1)}, u32[]{:S(2)}, u32[]{:S(2)}) async-start(bf16[16,16,512]{2,1,0:T(8,128)(2,1)} %get-tuple-element.21), calls=%async_computation | async-start | bytes 524288 | tf_op jit(solution)/shard_map/all_to_all | solution.py:208
  18.0 1.9 collective-permute-start
  19.9 2.4 %collective-permute-start.1 = (bf16[2048,384]{1,0:T(8,128)(2,1)}, bf16[2048,384]{1,0:T(8,128)(2,1)}, u32[]{:S(2)}, u32[]{:S(2)}) collective-permute-start(bf16[2048,384]{1,0:T(8,128)(2,1)} %bitcast.17), channel_id=1, source_target_pairs={{0,4},{4,0},{1,5},{5,1},{2,6},{6,2},{3,7},{7,3},{8,12},{12,8},{9,1... | collective-permute-start | bytes 4718600 | tf_op jit(solution)/shard_map/ppermute | solution.py:226
  22.3 1.9 collective-permute-start.2
  24.2 0.0 copy-start.4
  24.2 0.7 copy-done.4
  24.9 0.7 copy-done.5
  25.6 0.7 copy-done.6
  26.3 0.3 shard_map.96
  26.6 0.7 copy-done.2
  27.3 8.6 %all-to-all-done.r_ref = bf16[16,16,512]{2,1,0:T(8,128)(2,1)S(1)} async-done(((bf16[16,16,512]{2,1,0:T(8,128)(2,1)}), bf16[16,16,512]{2,1,0:T(8,128)(2,1)S(1)}, u32[]{:S(2)}, u32[]{:S(2)}) %all-to-all-start) | async-done | bytes 262176 | tf_op jit(solution)/shard_map/all_to_all | solution.py:208
  35.9 1.3 shard_map.97
  37.2 7.2 %all-to-all-start.1 = ((bf16[16,64,512]{2,1,0:T(8,128)(2,1)}), bf16[16,64,512]{2,1,0:T(8,128)(2,1)}, u32[]{:S(2)}, u32[]{:S(2)}) async-start(bf16[16,64,512]{2,1,0:T(8,128)(2,1)} %bitcast.28), calls=%async_computation.1 | async-start | bytes 2097152 | tf_op jit(solution)/shard_map/all_to_all | solution.py:213
  44.4 0.0 collective-permute-done.refs_1_
  44.4 0.0 collective-permute-done.2.refs_3_
  44.4 16.5 %all-to-all-done.1 = bf16[16,64,512]{2,1,0:T(8,128)(2,1)} async-done(((bf16[16,64,512]{2,1,0:T(8,128)(2,1)}), bf16[16,64,512]{2,1,0:T(8,128)(2,1)}, u32[]{:S(2)}, u32[]{:S(2)}) %all-to-all-start.1) | async-done | bytes 1048608 | tf_op jit(solution)/shard_map/all_to_all | solution.py:213
  60.9 4.0 %shard_map.98 = (bf16[4,4,64,512]{3,2,1,0:T(8,128)(2,1)S(1)}, f32[2,128,384]{2,1,0:T(8,128)S(1)}, f32[2,128,384]{2,1,0:T(8,128)S(1)}, bf16[384,2048]{1,0:T(8,128...) custom-call(bf16[2048,384]{1,0:T(8,128)(2,1)S(1)} %bitcast.15, ...), custom_call_target="tpu_custom_call" | custom-call | tf_op jit(solution)/shard_map/pallas_call | solution.py:40
  64.9 19.9 %all_to_all.45 = bf16[16,64,512]{2,1,0:T(8,128)(2,1)S(1)} all-to-all(bf16[16,64,512]{2,1,0:T(8,128)(2,1)S(1)} %bitcast.25), channel_id=1, replica_groups=mesh['y'=4,'z'=16,'c'=2,'h'=4] {'y','h'}, dimensions={0} | all-to-all | bytes 2097152 | tf_op jit(solution)/shard_map/all_to_all | solution.py:213
  84.8 0.3 shard_map.99
  85.1 24.4 %all_to_all.46.r_ref = bf16[16,16,512]{2,1,0:T(8,128)(2,1)S(1)} all-to-all(bf16[16,16,512]{2,1,0:T(8,128)(2,1)S(1)} %shard_map.99), channel_id=1, replica_groups=mesh['y'=4,'z'=16,'c'=2,'h'=4] {'z'}, dimensions={0} | all-to-all | bytes 524288 | tf_op jit(solution)/shard_map/all_to_all | solution.py:208
  109.5 1.0 shard_map.100
  110.5 7.7 %all_to_all.47.gram_ref = f32[4,8,128]{2,1,0:T(8,128)S(1)} all-to-all(f32[4,8,128]{2,1,0:T(8,128)S(1)} %get-tuple-element.30), channel_id=1, replica_groups=mesh['y'=4,'z'=16,'c'=2,'h'=4] {'h'}, dimensions={0} | all-to-all | bytes 32768 | tf_op jit(solution)/shard_map/all_to_all | solution.py:249
  118.2 0.4 shard_map.101
  118.6 20.6 %all_to_all.48.r_ref = bf16[16,16,512]{2,1,0:T(8,128)(2,1)S(1)} all-to-all(bf16[16,16,512]{2,1,0:T(8,128)(2,1)S(1)} %shard_map.101), channel_id=1, replica_groups=mesh['y'=4,'z'=16,'c'=2,'h'=4] {'z'}, dimensions={0} | all-to-all | bytes 524288 | tf_op jit(solution)/shard_map/all_to_all | solution.py:208
  139.1 0.2 shard_map.102
  139.4 16.3 %all_to_all.49 = bf16[16,64,512]{2,1,0:T(8,128)(2,1)S(1)} all-to-all(bf16[16,64,512]{2,1,0:T(8,128)(2,1)S(1)} %bitcast.23), channel_id=1, replica_groups=mesh['y'=4,'z'=16,'c'=2,'h'=4] {'y','h'}, dimensions={0} | all-to-all | bytes 2097152 | tf_op jit(solution)/shard_map/all_to_all | solution.py:213
  155.7 3.3 %shard_map.103 = bf16[4,4,64,512]{3,2,1,0:T(8,128)(2,1)S(1)} custom-call(bf16[4,4,64,512]{3,2,1,0:T(8,128)(2,1)S(1)} %bitcast.20, f32[2,128,384]{2,1,0:T(8,128)S(1)} %get-tuple-element.34.dgate_ref, f32[2,128,384]{2,1,0:T(8,128)S(1)} %get-tuple-element.35.dup_ref, bf16[2048,384]{1,0:T(8,128)(2,1)S(1)} %bitcast.16, bf16[2048,384]{1,0:T(8,128)(2,1)S(1)} %bitcast.19, ...), custom_call_target="tpu_custom_call" | custom-call | tf_op jit(solution)/shard_map/pallas_call | solution.py:40
  159.0 15.9 %all_to_all.50 = bf16[16,64,512]{2,1,0:T(8,128)(2,1)S(1)} all-to-all(bf16[16,64,512]{2,1,0:T(8,128)(2,1)S(1)} %bitcast.21), channel_id=1, replica_groups=mesh['y'=4,'z'=16,'c'=2,'h'=4] {'y','h'}, dimensions={0} | all-to-all | bytes 2097152 | tf_op jit(solution)/shard_map/all_to_all | solution.py:213
  174.8 0.3 shard_map.104
  175.1 22.5 %all_to_all.51.r_ref = bf16[16,16,512]{2,1,0:T(8,128)(2,1)S(1)} all-to-all(bf16[16,16,512]{2,1,0:T(8,128)(2,1)S(1)} %shard_map.104), channel_id=1, replica_groups=mesh['y'=4,'z'=16,'c'=2,'h'=4] {'z'}, dimensions={0} | all-to-all | bytes 524288 | tf_op jit(solution)/shard_map/all_to_all | solution.py:208
  197.6 0.9 shard_map.105
  (10 shorter events, 0.0 us)
Async XLA Ops:
  2.7 33.1 %all-to-all-start = ((bf16[16,16,512]{2,1,0:T(8,128)(2,1)}), bf16[16,16,512]{2,1,0:T(8,128)(2,1)S(1)}, u32[]{:S(2)}, u32[]{:S(2)}) async-start(bf16[16,16,512]{2,1,0:T(8,128)(2,1)} %get-tuple-element.21), calls=%async_computation | async-start | bytes 524288 | tf_op jit(solution)/shard_map/all_to_all | solution.py:208
  18.0 26.4 %collective-permute-start = (bf16[2048,384]{1,0:T(8,128)(2,1)}, bf16[2048,384]{1,0:T(8,128)(2,1)}, u32[]{:S(2)}, u32[]{:S(2)}) collective-permute-start(bf16[2048,384]{1,0:T(8,128)(2,1)} %bitcast.14), channel_id=1, source_target_pairs={{0,4},{4,0},{1,5},{5,1},{2,6},{6,2},{3,7},{7,3},{8,12},{12,8},{9,1... | collective-permute-start | bytes 4718600 | tf_op jit(solution)/shard_map/ppermute | solution.py:226
  19.9 24.5 %collective-permute-start.1 = (bf16[2048,384]{1,0:T(8,128)(2,1)}, bf16[2048,384]{1,0:T(8,128)(2,1)}, u32[]{:S(2)}, u32[]{:S(2)}) collective-permute-start(bf16[2048,384]{1,0:T(8,128)(2,1)} %bitcast.17), channel_id=1, source_target_pairs={{0,4},{4,0},{1,5},{5,1},{2,6},{6,2},{3,7},{7,3},{8,12},{12,8},{9,1... | collective-permute-start | bytes 4718600 | tf_op jit(solution)/shard_map/ppermute | solution.py:226
  22.3 22.1 %collective-permute-start.2 = (bf16[384,2048]{1,0:T(8,128)(2,1)}, bf16[384,2048]{1,0:T(8,128)(2,1)}, u32[]{:S(2)}, u32[]{:S(2)}) collective-permute-start(bf16[384,2048]{1,0:T(8,128)(2,1)} %bitcast.29), channel_id=1, source_target_pairs={{0,4},{4,0},{1,5},{5,1},{2,6},{6,2},{3,7},{7,3},{8,12},{12,8},{9,1... | collective-permute-start | bytes 4718600 | tf_op jit(solution)/shard_map/ppermute | solution.py:226
  24.2 0.7 copy-start.4
  24.9 0.7 copy-start.5
  25.6 0.7 copy-start.6
  26.6 0.7 copy-start.2
  35.9 25.0 %copy-start = (bf16[1,2048,384]{2,1,0:T(8,128)(2,1)S(1)}, bf16[1,2048,384]{2,1,0:T(8,128)(2,1)}, u32[]{:S(2)}) copy-start(bf16[1,2048,384]{2,1,0:T(8,128)(2,1)} %param.13) | copy-start | bytes 4718596
  35.9 25.0 %copy-start.1 = (bf16[1,2048,384]{2,1,0:T(8,128)(2,1)S(1)}, bf16[1,2048,384]{2,1,0:T(8,128)(2,1)}, u32[]{:S(2)}) copy-start(bf16[1,2048,384]{2,1,0:T(8,128)(2,1)} %param.14) | copy-start | bytes 4718596
  37.2 23.8 %all-to-all-start.1 = ((bf16[16,64,512]{2,1,0:T(8,128)(2,1)}), bf16[16,64,512]{2,1,0:T(8,128)(2,1)}, u32[]{:S(2)}, u32[]{:S(2)}) async-start(bf16[16,64,512]{2,1,0:T(8,128)(2,1)} %bitcast.28), calls=%async_computation.1 | async-start | bytes 2097152 | tf_op jit(solution)/shard_map/all_to_all | solution.py:213
  84.8 33.4 %copy-start.3 = (f32[128,512]{1,0:T(8,128)S(1)}, f32[128,512]{1,0:T(8,128)}, u32[]{:S(2)}) copy-start(f32[128,512]{1,0:T(8,128)} %copy-done.2) | copy-start | bytes 786436

commit v5 on v4

--- a/solution.py
+++ b/solution.py
@@ -51,7 +51,7 @@
     return (iota((PAIRS, TOK), 0) >> 3) == iota((PAIRS, TOK), 1)
 
 
-def place_body(tok_hbm, ids_hbm, out_ref, pm_ref, tok_ref, ids_ref, sems):
+def place_body(tok_hbm, ids_hbm, out_ref, pm_ref, turned_ref, tok_ref, ids_ref, sems):
     copies = [pltpu.make_async_copy(ids_hbm, ids_ref, sems.at[0]), pltpu.make_async_copy(tok_hbm, tok_ref, sems.at[1])]
     for c in copies:
         c.start()
@@ -63,19 +63,25 @@
     ids_col = jnp.sum(jnp.where(iota((PAIRS, TOPK), 1) == (pair & 7), tall, 0.0), axis=1, keepdims=True)
     flat = dot(ids, repeat, ((1,), (1,)))
     ids_row = jnp.sum(jnp.where(iota((TOPK, PAIRS), 0) == (lane & 7), flat, 0.0), axis=0, keepdims=True)
-    before = (ids_col == ids_row) & ((lane >> 3) < (pair >> 3))
-    slot = jnp.sum(jnp.where(before, 1.0, 0.0), axis=1, keepdims=True)
-    row = iota((1, ROWS), 1)
-    other = ((row >> 1) + lax.axis_index("c")) & 1
-    expert = ((((row >> 2) & 3) * NZ + (row >> 4)) * NC + other).astype(F32)
-    pm = one_hot((expert == ids_col) & ((row & 1).astype(F32) == slot))
-    pm_ref[...] = pm
-    pick = dot(pm, repeat, ((0,), (0,))).astype(BF16)
+    same = ids_col == ids_row
+    slot_row = jnp.sum(jnp.where(same & ((pair >> 3) < (lane >> 3)), 1.0, 0.0), axis=0, keepdims=True)
+
+    def bucket(row):
+        expert = (((row >> 2) & 3) * NZ + (row >> 4)) * NC + (((row >> 1) + lax.axis_index("c")) & 1)
+        return expert.astype(F32), (row & 1).astype(F32)
+
+    expert, place = bucket(iota((ROWS, 1), 0))
+    turned = one_hot((expert == ids_row) & (place == slot_row))
+    turned_ref[...] = turned
+    pick = dot(turned, repeat).astype(BF16)
+    slot = jnp.sum(jnp.where(same & ((lane >> 3) < (pair >> 3)), 1.0, 0.0), axis=1, keepdims=True)
+    expert, place = bucket(iota((1, ROWS), 1))
+    pm_ref[...] = one_hot((expert == ids_col) & (place == slot))
     copies[1].wait()
     out_ref[...] = dot(pick, tok_ref[...]).astype(BF16).reshape(NZ, 16, PART)
 
 
-def home_body(probs_ref, pad_ref, up_ref, share_ref, su_ref, mask_ref):
+def home_body(probs_ref, pad_ref, up_ref, pm_ref, pick_ref, share_ref, su_ref, mask_ref):
     pair, lane = iota((PAIRS, 1), 0), iota((1, PAIRS), 1)
     owner = owners()
     repeat = one_hot(owner)
@@ -90,6 +96,7 @@
     share_row = jnp.sum(jnp.where(iota((TOPK, PAIRS), 0) == (lane & 7), share_flat, 0.0), axis=0, keepdims=True)
     share_ref[...] = jnp.where(iota((TOK, PAIRS), 0) == (iota((TOK, PAIRS), 1) >> 3), share_row, 0.0)
     su_ref[...] = (pad_col * share_col) * dot(repeat, up_ref[...])
+    pick_ref[...] = dot(one_hot(iota((TOK, PAIRS), 0) == (iota((TOK, PAIRS), 1) >> 3)), pm_ref[...]).astype(BF16)
     same = ((lane >> 3) == (pair >> 3)) & (lane != pair)
     mask_ref[...] = jnp.where(same, pad_col * (orth_weight / math.sqrt(WIDE)), 0.0)
 
@@ -190,18 +197,16 @@
     layer_ref[...] = fine_dot(share_ref[...], out).astype(BF16)
 
 
-def grad_body(gram_ref, out_ref, su_ref, mask_ref, pm_ref, rows_ref):
+def grad_body(gram_ref, out_ref, su_ref, mask_ref, turned_ref, rows_ref):
     packed = (gram_ref[0] + gram_ref[1]) + (gram_ref[2] + gram_ref[3])
     full = jnp.broadcast_to(packed[None], (TOK, TOPK, PAIRS)).reshape(PAIRS, PAIRS)
     grad = su_ref[...] + fine_dot(full * mask_ref[...], out_ref[...])
-    rows = dot(pm_ref[...], grad.astype(BF16), ((0,), (0,))).astype(BF16)
+    rows = dot(turned_ref[...], grad.astype(BF16)).astype(BF16)
     rows_ref[...] = rows.reshape(NZ, 16, PART)
 
 
-def combine_body(r_ref, pm_ref, out_ref):
-    repeat = one_hot(iota((TOK, PAIRS), 0) == (iota((TOK, PAIRS), 1) >> 3))
-    pick = dot(repeat, pm_ref[...]).astype(BF16)
-    out_ref[...] = dot(pick, r_ref[...].reshape(ROWS, PART)).astype(BF16)
+def combine_body(r_ref, pick_ref, out_ref):
+    out_ref[...] = dot(pick_ref[...], r_ref[...].reshape(ROWS, PART)).astype(BF16)
 
 
 def over_z(x):
@@ -218,18 +223,19 @@
     plane = ((NY, NH, 64, PART), BF16)
     ring = ((NZ, 16, PART), BF16)
     hidden = ((2, HALF, own[0].shape[1]), F32)
-    placed, pm = call(
-        place_body, [ring, ((PAIRS, ROWS), BF16)], remote=(tokens, expert_ids.T), spaces=(pltpu.HBM, pltpu.VMEM),
+    placed, pm, turned = call(
+        place_body, [ring, ((PAIRS, ROWS), BF16), ((ROWS, PAIRS), BF16)], remote=(tokens, expert_ids.T),
+        spaces=(pltpu.HBM, pltpu.VMEM, pltpu.VMEM),
         scratch=[pltpu.VMEM((TOK, PART), BF16), pltpu.VMEM((TOPK, TOK), jnp.int32), pltpu.SemaphoreType.DMA((2,))],
     )
     rows = over_z(placed)
     swapped = [lax.ppermute(w, "c", [(0, 1), (1, 0)]) for w in own]
     known = call(
         home_body,
-        [((TOK, PAIRS), F32), ((PAIRS, PART), F32), ((PAIRS, PAIRS), F32)],
-        gate_probs.T, pad_mask.reshape(1, TOK), upstream, spaces=(pltpu.VMEM,) * 3,
-    )
-    rows, (share, su, mask) = lax.optimization_barrier((rows, known))
+        [((TOK, ROWS), BF16), ((TOK, PAIRS), F32), ((PAIRS, PART), F32), ((PAIRS, PAIRS), F32)],
+        gate_probs.T, pad_mask.reshape(1, TOK), upstream, pm, spaces=(pltpu.VMEM,) * 4,
+    )
+    rows, (pick, share, su, mask) = lax.optimization_barrier((rows, known))
     (spread,) = call(
         spread_out_body, [plane], rows, spaces=(pltpu.HBM,), scratch=[pltpu.VMEM((NY, 64, PART), BF16), pltpu.SemaphoreType.DMA((NH,))],
     )
@@ -247,13 +253,13 @@
         over_z(summed), pm, share,
     )
     gram = lax.all_to_all(gram, "h", 0, 0, tiled=True)
-    (grad_rows,) = call(grad_body, [ring], gram, out, su, mask, pm)
+    (grad_rows,) = call(grad_body, [ring], gram, out, su, mask, turned)
     (spread,) = call(spread_body, [plane], over_z(grad_rows))
     (partial,) = call(
         backward_body, [plane], over_plane(spread), dgate, dup, own[0], own[1], *late, vmem=24 << 20,
     )
     (summed,) = call(reduce_body, [ring], over_plane(partial))
-    (grad_tokens,) = call(combine_body, [((TOK, PART), BF16)], over_z(summed), pm)
+    (grad_tokens,) = call(combine_body, [((TOK, PART), BF16)], over_z(summed), pick)
     return (layer_out, grad_tokens)
 
 

time: 199 us -> 199 us (level)
  no operation moved by 1% of the time
where the time goes in v5:
time: 199 us; the launch traced here: 198 us
  blocking collectives  127 us (64%)
  starting transfers between devices  28.7 us (14%)
  waiting for transfers between devices  24.4 us (12%)
  Pallas kernels  13.9 us (7%)
  local copies, waits for them, and re-layouts  3.4 us (2%)
    all_to_all x3, blocking collectives, over_z(): return lax.all_to_all(x, 'z', 0, 0, tiled=True)  67.4 us
    all_to_all x3, blocking collectives, over_plane(): lax.all_to_all(x.reshape(NY * NH, 64, PART), ('y', 'h'), 0, 0, tiled=True)  52 us
    all_to_all x1, waiting for transfers between devices, over_plane(): lax.all_to_all(x.reshape(NY * NH, 64, PART), ('y', 'h'), 0, 0, tiled=True)  16.5 us
    all_to_all x1, starting transfers between devices, over_z(): return lax.all_to_all(x, 'z', 0, 0, tiled=True)  15.2 us
    pallas_call x11, Pallas kernels, call(): pl.pallas_call(body, out_shape=[make(*out) for make, out in zip(spaces or...  13.9 us
    all_to_all x1, waiting for transfers between devices, over_z(): return lax.all_to_all(x, 'z', 0, 0, tiled=True)  7.91 us
    all_to_all x1, blocking collectives, shards(): gram = lax.all_to_all(gram, 'h', 0, 0, tiled=True)  7.7 us
    all_to_all x1, starting transfers between devices, over_plane(): lax.all_to_all(x.reshape(NY * NH, 64, PART), ('y', 'h'), 0, 0, tiled=True)  7.23 us
  transfers between devices with their start and end apart: 5, of which 2 were waited for; matrix products, arithmetic and copies ran while one was open for 0% of the time, Pallas kernels for 1%

profile of v5, /device:TPU:32, one launch (start us, length us, event | category | flops | bytes accessed | tf_op | source)
XLA Modules:
  0.0 198.3 jit_solution(15284060146228192775)
XLA Ops:
  0.6 2.0 %shard_map.95 = (bf16[16,16,512]{2,1,0:T(8,128)(2,1)}, bf16[128,256]{1,0:T(8,128)(2,1)S(1)}, bf16[256,128]{1,0:T(8,128)(2,1)S(1)}) custom-call(bf16[16,512]{1,0:T(8,128)(2,1)} %tok_hbm.1, s32[8,16]{1,0:T(8,128)} %bitcast.31), custom_call_target="tpu_custom_call" | custom-call | tf_op jit(solution)/shard_map/pallas_call | solution.py:40
  2.6 15.2 %all-to-all-start = ((bf16[16,16,512]{2,1,0:T(8,128)(2,1)}), bf16[16,16,512]{2,1,0:T(8,128)(2,1)S(1)}, u32[]{:S(2)}, u32[]{:S(2)}) async-start(bf16[16,16,512]{2,1,0:T(8,128)(2,1)} %get-tuple-element.24), calls=%async_computation | async-start | bytes 524288 | tf_op jit(solution)/shard_map/all_to_all | solution.py:213
  17.9 1.9 collective-permute-start
  19.8 2.4 %collective-permute-start.1 = (bf16[2048,384]{1,0:T(8,128)(2,1)}, bf16[2048,384]{1,0:T(8,128)(2,1)}, u32[]{:S(2)}, u32[]{:S(2)}) collective-permute-start(bf16[2048,384]{1,0:T(8,128)(2,1)} %bitcast.17), channel_id=1, source_target_pairs={{0,4},{4,0},{1,5},{5,1},{2,6},{6,2},{3,7},{7,3},{8,12},{12,8},{9,1... | collective-permute-start | bytes 4718600 | tf_op jit(solution)/shard_map/ppermute | solution.py:232
  22.2 1.9 collective-permute-start.2
  24.1 0.0 copy-start.6
  24.1 0.7 copy-done.6
  24.9 0.7 copy-done.7
  25.5 0.7 copy-done.8
  26.2 0.3 shard_map.96
  26.5 0.7 copy-done.2
  27.2 0.6 copy-done.4
  27.9 7.9 %all-to-all-done.r_ref = bf16[16,16,512]{2,1,0:T(8,128)(2,1)S(1)} async-done(((bf16[16,16,512]{2,1,0:T(8,128)(2,1)}), bf16[16,16,512]{2,1,0:T(8,128)(2,1)S(1)}, u32[]{:S(2)}, u32[]{:S(2)}) %all-to-all-start) | async-done | bytes 262176 | tf_op jit(solution)/shard_map/all_to_all | solution.py:213
  35.8 1.3 shard_map.97
  37.0 7.2 %all-to-all-start.1 = ((bf16[16,64,512]{2,1,0:T(8,128)(2,1)}), bf16[16,64,512]{2,1,0:T(8,128)(2,1)}, u32[]{:S(2)}, u32[]{:S(2)}) async-start(bf16[16,64,512]{2,1,0:T(8,128)(2,1)} %bitcast.28), calls=%async_computation.1 | async-start | bytes 2097152 | tf_op jit(solution)/shard_map/all_to_all | solution.py:218
  44.3 0.0 collective-permute-done.refs_1_
  44.3 16.5 %all-to-all-done.1 = bf16[16,64,512]{2,1,0:T(8,128)(2,1)} async-done(((bf16[16,64,512]{2,1,0:T(8,128)(2,1)}), bf16[16,64,512]{2,1,0:T(8,128)(2,1)}, u32[]{:S(2)}, u32[]{:S(2)}) %all-to-all-start.1) | async-done | bytes 1048608 | tf_op jit(solution)/shard_map/all_to_all | solution.py:218
  60.8 4.0 %shard_map.98 = (bf16[4,4,64,512]{3,2,1,0:T(8,128)(2,1)S(1)}, f32[2,128,384]{2,1,0:T(8,128)S(1)}, f32[2,128,384]{2,1,0:T(8,128)S(1)}, bf16[384,2048]{1,0:T(8,128...) custom-call(bf16[2048,384]{1,0:T(8,128)(2,1)S(1)} %bitcast.15, ...), custom_call_target="tpu_custom_call" | custom-call | tf_op jit(solution)/shard_map/pallas_call | solution.py:40
  64.8 19.9 %all_to_all.45 = bf16[16,64,512]{2,1,0:T(8,128)(2,1)S(1)} all-to-all(bf16[16,64,512]{2,1,0:T(8,128)(2,1)S(1)} %bitcast.25), channel_id=1, replica_groups=mesh['y'=4,'z'=16,'c'=2,'h'=4] {'y','h'}, dimensions={0} | all-to-all | bytes 2097152 | tf_op jit(solution)/shard_map/all_to_all | solution.py:218
  84.7 0.3 shard_map.99
  85.0 24.4 %all_to_all.46.r_ref = bf16[16,16,512]{2,1,0:T(8,128)(2,1)S(1)} all-to-all(bf16[16,16,512]{2,1,0:T(8,128)(2,1)S(1)} %shard_map.99), channel_id=1, replica_groups=mesh['y'=4,'z'=16,'c'=2,'h'=4] {'z'}, dimensions={0} | all-to-all | bytes 524288 | tf_op jit(solution)/shard_map/all_to_all | solution.py:213
  109.4 1.0 shard_map.100
  110.4 7.7 %all_to_all.47.gram_ref = f32[4,8,128]{2,1,0:T(8,128)S(1)} all-to-all(f32[4,8,128]{2,1,0:T(8,128)S(1)} %get-tuple-element.34), channel_id=1, replica_groups=mesh['y'=4,'z'=16,'c'=2,'h'=4] {'h'}, dimensions={0} | all-to-all | bytes 32768 | tf_op jit(solution)/shard_map/all_to_all | solution.py:255
  118.1 0.4 shard_map.101
  118.5 20.6 %all_to_all.48.r_ref = bf16[16,16,512]{2,1,0:T(8,128)(2,1)S(1)} all-to-all(bf16[16,16,512]{2,1,0:T(8,128)(2,1)S(1)} %shard_map.101), channel_id=1, replica_groups=mesh['y'=4,'z'=16,'c'=2,'h'=4] {'z'}, dimensions={0} | all-to-all | bytes 524288 | tf_op jit(solution)/shard_map/all_to_all | solution.py:213
  139.1 0.2 shard_map.102
  139.3 16.3 %all_to_all.49 = bf16[16,64,512]{2,1,0:T(8,128)(2,1)S(1)} all-to-all(bf16[16,64,512]{2,1,0:T(8,128)(2,1)S(1)} %bitcast.23), channel_id=1, replica_groups=mesh['y'=4,'z'=16,'c'=2,'h'=4] {'y','h'}, dimensions={0} | all-to-all | bytes 2097152 | tf_op jit(solution)/shard_map/all_to_all | solution.py:218
  155.6 3.3 %shard_map.103 = bf16[4,4,64,512]{3,2,1,0:T(8,128)(2,1)S(1)} custom-call(bf16[4,4,64,512]{3,2,1,0:T(8,128)(2,1)S(1)} %bitcast.20, f32[2,128,384]{2,1,0:T(8,128)S(1)} %get-tuple-element.39.dgate_ref, f32[2,128,384]{2,1,0:T(8,128)S(1)} %get-tuple-element.40.dup_ref, bf16[2048,384]{1,0:T(8,128)(2,1)S(1)} %bitcast.16, bf16[2048,384]{1,0:T(8,128)(2,1)S(1)} %bitcast.19, ...), custom_call_target="tpu_custom_call" | custom-call | tf_op jit(solution)/shard_map/pallas_call | solution.py:40
  158.9 15.8 %all_to_all.50 = bf16[16,64,512]{2,1,0:T(8,128)(2,1)S(1)} all-to-all(bf16[16,64,512]{2,1,0:T(8,128)(2,1)S(1)} %bitcast.21), channel_id=1, replica_groups=mesh['y'=4,'z'=16,'c'=2,'h'=4] {'y','h'}, dimensions={0} | all-to-all | bytes 2097152 | tf_op jit(solution)/shard_map/all_to_all | solution.py:218
  174.7 0.3 shard_map.104
  175.0 22.5 %all_to_all.51.r_ref = bf16[16,16,512]{2,1,0:T(8,128)(2,1)S(1)} all-to-all(bf16[16,16,512]{2,1,0:T(8,128)(2,1)S(1)} %shard_map.104), channel_id=1, replica_groups=mesh['y'=4,'z'=16,'c'=2,'h'=4] {'z'}, dimensions={0} | all-to-all | bytes 524288 | tf_op jit(solution)/shard_map/all_to_all | solution.py:213
  197.5 0.8 shard_map.105
  (14 shorter events, 0.0 us)
Async XLA Ops:
  2.6 33.1 %all-to-all-start = ((bf16[16,16,512]{2,1,0:T(8,128)(2,1)}), bf16[16,16,512]{2,1,0:T(8,128)(2,1)S(1)}, u32[]{:S(2)}, u32[]{:S(2)}) async-start(bf16[16,16,512]{2,1,0:T(8,128)(2,1)} %get-tuple-element.24), calls=%async_computation | async-start | bytes 524288 | tf_op jit(solution)/shard_map/all_to_all | solution.py:213
  17.9 26.4 %collective-permute-start = (bf16[2048,384]{1,0:T(8,128)(2,1)}, bf16[2048,384]{1,0:T(8,128)(2,1)}, u32[]{:S(2)}, u32[]{:S(2)}) collective-permute-start(bf16[2048,384]{1,0:T(8,128)(2,1)} %bitcast.14), channel_id=1, source_target_pairs={{0,4},{4,0},{1,5},{5,1},{2,6},{6,2},{3,7},{7,3},{8,12},{12,8},{9,1... | collective-permute-start | bytes 4718600 | tf_op jit(solution)/shard_map/ppermute | solution.py:232
  19.8 24.5 %collective-permute-start.1 = (bf16[2048,384]{1,0:T(8,128)(2,1)}, bf16[2048,384]{1,0:T(8,128)(2,1)}, u32[]{:S(2)}, u32[]{:S(2)}) collective-permute-start(bf16[2048,384]{1,0:T(8,128)(2,1)} %bitcast.17), channel_id=1, source_target_pairs={{0,4},{4,0},{1,5},{5,1},{2,6},{6,2},{3,7},{7,3},{8,12},{12,8},{9,1... | collective-permute-start | bytes 4718600 | tf_op jit(solution)/shard_map/ppermute | solution.py:232
  22.2 22.1 %collective-permute-start.2 = (bf16[384,2048]{1,0:T(8,128)(2,1)}, bf16[384,2048]{1,0:T(8,128)(2,1)}, u32[]{:S(2)}, u32[]{:S(2)}) collective-permute-start(bf16[384,2048]{1,0:T(8,128)(2,1)} %bitcast.29), channel_id=1, source_target_pairs={{0,4},{4,0},{1,5},{5,1},{2,6},{6,2},{3,7},{7,3},{8,12},{12,8},{9,1... | collective-permute-start | bytes 4718600 | tf_op jit(solution)/shard_map/ppermute | solution.py:232
  24.1 0.7 copy-start.6
  24.8 0.7 copy-start.7
  25.5 0.7 copy-start.8
  26.5 0.7 copy-start.2
  27.2 0.6 copy-start.4
  35.8 25.1 %copy-start = (bf16[1,2048,384]{2,1,0:T(8,128)(2,1)S(1)}, bf16[1,2048,384]{2,1,0:T(8,128)(2,1)}, u32[]{:S(2)}) copy-start(bf16[1,2048,384]{2,1,0:T(8,128)(2,1)} %param.13) | copy-start | bytes 4718596
  35.8 25.1 %copy-start.1 = (bf16[1,2048,384]{2,1,0:T(8,128)(2,1)S(1)}, bf16[1,2048,384]{2,1,0:T(8,128)(2,1)}, u32[]{:S(2)}) copy-start(bf16[1,2048,384]{2,1,0:T(8,128)(2,1)} %param.14) | copy-start | bytes 4718596
  37.0 23.8 %all-to-all-start.1 = ((bf16[16,64,512]{2,1,0:T(8,128)(2,1)}), bf16[16,64,512]{2,1,0:T(8,128)(2,1)}, u32[]{:S(2)}, u32[]{:S(2)}) async-start(bf16[16,64,512]{2,1,0:T(8,128)(2,1)} %bitcast.28), calls=%async_computation.1 | async-start | bytes 2097152 | tf_op jit(solution)/shard_map/all_to_all | solution.py:218
  84.7 33.4 %copy-start.3 = (f32[128,512]{1,0:T(8,128)S(1)}, f32[128,512]{1,0:T(8,128)}, u32[]{:S(2)}) copy-start(f32[128,512]{1,0:T(8,128)} %copy-done.2) | copy-start | bytes 786436
  84.7 33.4 %copy-start.5 = (f32[128,128]{1,0:T(8,128)S(1)}, f32[128,128]{1,0:T(8,128)}, u32[]{:S(2)}) copy-start(f32[128,128]{1,0:T(8,128)} %copy-done.4) | copy-start | bytes 196612
